TPU v7x, 32 devices: a whole 2x2x4 slice. The times are simulated.
32 devices in a mesh: cells: 8 (over z, x), tm: 4 (over y, core).
Axes of the slice: x: 2, y: 2, z: 4, core: 2. Of those that a mesh axis runs over, the one named last changes fastest.
Arguments:
- geopotential: bfloat16 [10240, 4096], P('tm', 'cells'), may hold values from -16 to 16
- meridional: bfloat16 [10240, 4096], P('tm', 'cells'), may hold values from -16 to 16
- day_index: int32 [10240], P('tm'), may hold values from 0 to 364, as said below
Outputs:
- eddy_climate: float32 [3, 365, 4096], P(None, None, 'cells')
- zonal_climate: float32 [3, 365, 128], replicated
Inputs may be any that keep to these rules, and one draw needn't show every extreme that they name: `day_index`: consecutive daily frames of a calendar with a leap year every fourth year, in which February 29 shares the bin of February 28; every bin occurs.
All inputs are finite; a program needn't handle non-finite values.
Results may differ from a plain program's by a relative error of at most 0.00063.
The roundings to bfloat16 on the way count: a program that leaves them out, or rounds other values in their place, can miss the bound.
Values may be sent and summed in bfloat16 or wider, within the bound.
A program may use at most 128 MiB of HBM per device.

v0:
```python
import jax
import jax.numpy as jnp
from jax import lax
from jax.sharding import PartitionSpec as P

LAT = 128
HALF = 15
WIN = 7
DAYS = 365


def extended(shard, sides, width):
    for axis, dim in sides:
        size, length = (lax.axis_size(axis), shard.shape[dim])
        up = [(i, (i + 1) % size) for i in range(size - 1)]
        down = [(j, i) for i, j in up]
        last = lax.slice_in_dim(shard, length - width, length, axis=dim)
        initial = lax.slice_in_dim(shard, 0, width, axis=dim)
        before = lax.ppermute(last, axis, up)
        after = lax.ppermute(initial, axis, down)
        shard = jnp.concatenate([before, shard, after], axis=dim)
    return shard


def lanczos_tap(offset):
    nonzero = jnp.where(offset == 0, 1.0, offset)
    response = (jnp.sin(jnp.pi * nonzero) - jnp.sin(0.25 * jnp.pi * nonzero)) / (jnp.pi * nonzero)
    smoother = jnp.sin(jnp.pi * nonzero / (HALF + 1)) / (jnp.pi * nonzero / (HALF + 1))
    return jnp.where(offset == 0, 0.75, response * smoother)


def window_matrix(distance):
    return (distance <= WIN) | (distance >= DAYS - WIN)


def calendar(padded, calendar_days, frames, cell_count):
    out_rows = jnp.arange(128, dtype=jnp.int32)[:, None]
    in_rows = jnp.arange(128 + 2 * HALF, dtype=jnp.int32)[None, :]
    offsets = in_rows - out_rows - HALF
    taps_matrix = jnp.where(
        jnp.abs(offsets) <= HALF, lanczos_tap(offsets.astype(jnp.float32)), 0.0
    ).astype(jnp.bfloat16)
    day_axis = jnp.arange(DAYS, dtype=jnp.int32)[:, None]

    def advance(number, running):
        totals, tallies = running
        offset = number * 512
        segment = lax.dynamic_slice_in_dim(padded, offset, 512 + 2 * HALF, 1)
        tile_stack = jnp.stack(
            [
                segment[:, tile_index * 128 : tile_index * 128 + 128 + 2 * HALF]
                for tile_index in range(4)
            ],
            axis=1,
        )
        filtered = jnp.einsum(
            "ik,fjkc->fjic", taps_matrix, tile_stack, preferred_element_type=jnp.float32
        ).reshape(2, 512, cell_count)
        height = filtered[0]
        meridional_f = filtered[1]
        products = jnp.stack(
            [height * height, meridional_f * meridional_f, height * meridional_f]
        ).astype(jnp.bfloat16)
        block_days = lax.dynamic_slice_in_dim(calendar_days, offset, 512)
        distance = (day_axis - block_days[None, :]) % DAYS
        inside = window_matrix(distance)
        totals = totals + jnp.einsum(
            "dt,stc->sdc", inside.astype(jnp.bfloat16), products, preferred_element_type=jnp.float32
        )
        tallies = tallies + jnp.sum(inside.astype(jnp.float32), axis=1)
        return (totals, tallies)

    initial = (jnp.zeros((3, DAYS, cell_count), jnp.float32), jnp.zeros((DAYS,), jnp.float32))
    return lax.fori_loop(0, frames // 512, advance, initial)


def smooth_days(totals, tallies):
    result = (totals, tallies)
    return result


def local(geopotential, meridional, day_index):
    frames, cell_count = geopotential.shape
    longitudes = cell_count // LAT
    lon_total = longitudes * lax.axis_size("cells")
    stacked = jnp.stack([geopotential, meridional])
    partial_value = jnp.sum(stacked.reshape(2, frames, longitudes, LAT), axis=2, dtype=jnp.float32)
    zonal_mean = lax.psum(partial_value, "cells") / lon_total
    anomaly = (stacked.astype(jnp.float32) - jnp.tile(zonal_mean, (1, 1, longitudes))).astype(
        jnp.bfloat16
    )
    padded = extended(anomaly, (("tm", 1),), HALF)
    totals, tallies = calendar(padded, day_index, frames, cell_count)
    totals, tallies = lax.psum((totals, tallies), "tm")
    totals, tallies = smooth_days(totals, tallies)
    climate = totals / tallies[None, :, None]
    zonal_part = jnp.sum(climate.reshape(3, DAYS, longitudes, LAT), axis=2)
    zonal_climate = lax.psum(zonal_part, "cells") / lon_total
    return (climate, zonal_climate)


def solution(mesh):
    return jax.shard_map(
        local,
        mesh=mesh,
        in_specs=(P("tm", "cells"), P("tm", "cells"), P("tm")),
        out_specs=(P(None, None, "cells"), P()),
        check_vma=False,
    )
```

profile of v0, /device:TPU:1, one launch (start us, length us, event | category | flops | bytes accessed | tf_op | source)
XLA Modules:
  0.0 410.4 jit_solution(15855096080680505465)
XLA Ops:
  7.2 5.0 %stack.88 = bf16[1,2560,4,128]{3,2,1,0:T(4,128)(2,1)} reshape(bf16[2560,512]{1,0:T(8,128)(2,1)} %param.5) | data formatting | bytes 5242880 | tf_op jit(solution)/shard_map/stack | solution.py:86
  12.3 2.8 stack.89
  15.1 29.8 %convert_reduce_fusion.1 = f32[2,2560,128]{2,1,0:T(8,128)} fusion(bf16[1,2560,4,128]{3,2,1,0:T(4,128)(2,1)} %stack.89, bf16[1,2560,4,128]{3,2,1,0:T(4,128)(2,1)} %stack.88), kind=kLoop, calls=%fused_computation.68 | loop fusion | flops 7208960 | bytes 7864320 | tf_op jit(solution)/shard_map/reduce_sum | solution.py:87
  44.9 117.0 %all-reduce.4.cloned.1.call-done = f32[2,2560,128]{2,1,0:T(8,128)} async-done(((f32[2,2560,128]{2,1,0:T(8,128)}), f32[2,2560,128]{2,1,0:T(8,128)}) %all-reduce.4.cloned.1.call-update) | async-done | bytes 2621456 | tf_op jit(solution)/shard_map/psum | solution.py:88
  161.9 1.9 broadcast_multiply_fusion
  163.9 5.1 %tile.4 = f32[2,2560,4,128]{3,2,1,0:T(4,128)} broadcast(f32[2,2560,128]{2,1,0:T(8,128)S(1)} %broadcast_multiply_fusion), dimensions={0,1,3} | broadcast | bytes 13107200 | tf_op jit(solution)/shard_map/tile | solution.py:89
  169.0 12.7 %tile.10 = f32[2,2560,512]{2,1,0:T(8,128)} reshape(f32[2,2560,4,128]{3,2,1,0:T(4,128)} %tile.4) | data formatting | bytes 20971520 | tf_op jit(solution)/shard_map/tile | solution.py:89
  181.7 8.9 %subtract_convert_fusion = bf16[2,2560,512]{2,1,0:T(8,128)(2,1)} fusion(f32[2,2560,512]{2,1,0:T(8,128)} %tile.10, bf16[1,2560,512]{2,1,0:T(8,128)(2,1)S(1)} %bitcast.50, bf16[1,2560,512]{2,1,0:T(8,128)(2,1)} %bitcast.51), kind=kLoop, calls=%fused_computation.67 | loop fusion | flops 10485760 | bytes 20971520 | tf_op jit(solution)/shard_map/convert_element_type | solution.py:89
  191.4 4.6 %collective-permute-start = (bf16[2,15,512]{2,1,0:T(8,128)(2,1)S(1)}, bf16[2,15,512]{2,1,0:T(8,128)(2,1)S(1)}, u32[]{:S(2)}, u32[]{:S(2)}) collective-permute-start(bf16[2,15,512]{2,1,0:T(8,128)(2,1)S(1)} %get-tuple-element.222), channel_id=1, source_target_pairs={{0,1},{1,2},{2,3},{4,5},{5,6},{6,7},{8,9},{9,10},{10,11},{12,13},{... | collective-permute-start | bytes 92168 | tf_op jit(solution)/shard_map/ppermute | solution.py:19
  196.0 2.1 collective-permute-start.1
  198.1 3.1 collective-permute-done.1
  201.2 27.2 %concatenate.4 = bf16[2,2590,512]{2,1,0:T(8,128)(2,1)} concatenate(bf16[2,15,512]{2,1,0:T(8,128)(2,1)S(1)} %collective-permute-done, bf16[2,2560,512]{2,1,0:T(8,128)(2,1)} %subtract_convert_fusion, bf16[2,15,512]{2,1,0:T(8,128)(2,1)S(1)} %collective-permute-done.1), dimensions={1} | concatenate | bytes 10608640 | tf_op jit(solution)/shard_map/concatenate | solution.py:21
  228.5 42.8 %while.18 = (s32[]{:T(128)}, f32[3,365,512]{2,1,0:T(8,128)}, f32[365]{0:T(512)S(1)}, bf16[2,2590,512]{2,1,0:T(8,128)(2,1)}, s32[2560]{0:T(1024)}, /*index=5*/s32...) while((s32[]{:T(128)}, f32[3,365,512]{2,1,0:T(8,128)}, ...), condition=%wide.region_4.5_spmd.clone, body=%wide.region_2.4_spmd.clone.sunk | while | flops 750434368 | bytes 15722455 | solution.py:74
  232.4 2.6 bitcast_add_fusion.2
  239.7 4.2 %bitcast_add_fusion.2 = f32[3,365,512]{2,1,0:T(8,128)} fusion(f32[3,365,512]{2,1,0:T(8,128)} %get-tuple-element.282, bf16[1,512,512]{2,1,0:T(8,128)(2,1)S(1)} %bitcast.48, bf16[1,512,512]{2,1,0:T(8,128)(2,1)S(1)} %bitcast.49, bf16[1,512,512]{2,1,0:T(8,128)(2,1)S(1)} %bitcast.47, pred[]{:T(512)S(6)} %compare.3, s32[512]{0:T(512)S(1)} %dynamic_slice.23), kind=kOutput, calls=%fused_computation.2.clone.1 | convolution fusion | flops 578658304 | bytes 6060033 | tf_op jit(solution)/shard_map/while/body/eval_jaxpr/dt,stc->sdc/dot_general | solution.py:67
  248.6 4.2 %bitcast_add_fusion.2 = f32[3,365,512]{2,1,0:T(8,128)} fusion(f32[3,365,512]{2,1,0:T(8,128)} %get-tuple-element.282, bf16[1,512,512]{2,1,0:T(8,128)(2,1)S(1)} %bitcast.48, bf16[1,512,512]{2,1,0:T(8,128)(2,1)S(1)} %bitcast.49, bf16[1,512,512]{2,1,0:T(8,128)(2,1)S(1)} %bitcast.47, pred[]{:T(512)S(6)} %compare.3, s32[512]{0:T(512)S(1)} %dynamic_slice.23), kind=kOutput, calls=%fused_computation.2.clone.1 | convolution fusion | flops 578658304 | bytes 6060033 | tf_op jit(solution)/shard_map/while/body/eval_jaxpr/dt,stc->sdc/dot_general | solution.py:67
  257.5 4.2 %bitcast_add_fusion.2 = f32[3,365,512]{2,1,0:T(8,128)} fusion(f32[3,365,512]{2,1,0:T(8,128)} %get-tuple-element.282, bf16[1,512,512]{2,1,0:T(8,128)(2,1)S(1)} %bitcast.48, bf16[1,512,512]{2,1,0:T(8,128)(2,1)S(1)} %bitcast.49, bf16[1,512,512]{2,1,0:T(8,128)(2,1)S(1)} %bitcast.47, pred[]{:T(512)S(6)} %compare.3, s32[512]{0:T(512)S(1)} %dynamic_slice.23), kind=kOutput, calls=%fused_computation.2.clone.1 | convolution fusion | flops 578658304 | bytes 6060033 | tf_op jit(solution)/shard_map/while/body/eval_jaxpr/dt,stc->sdc/dot_general | solution.py:67
  266.3 4.2 %bitcast_add_fusion.2 = f32[3,365,512]{2,1,0:T(8,128)} fusion(f32[3,365,512]{2,1,0:T(8,128)} %get-tuple-element.282, bf16[1,512,512]{2,1,0:T(8,128)(2,1)S(1)} %bitcast.48, bf16[1,512,512]{2,1,0:T(8,128)(2,1)S(1)} %bitcast.49, bf16[1,512,512]{2,1,0:T(8,128)(2,1)S(1)} %bitcast.47, pred[]{:T(512)S(6)} %compare.3, s32[512]{0:T(512)S(1)} %dynamic_slice.23), kind=kOutput, calls=%fused_computation.2.clone.1 | convolution fusion | flops 578658304 | bytes 6060033 | tf_op jit(solution)/shard_map/while/body/eval_jaxpr/dt,stc->sdc/dot_general | solution.py:67
  271.3 5.1 %psum.30 = f32[365]{0:T(512)S(1)} all-reduce(f32[365]{0:T(512)S(1)} %get-tuple-element.181), channel_id=1, replica_groups=mesh['cells'=8,'tm'=4] {'tm'}, use_global_device_ids=true, to_apply=%region_6.7 | all-reduce | flops 365 | bytes 2920 | tf_op jit(solution)/shard_map/psum | solution.py:94
  276.4 46.6 %all-reduce.6.cloned.1.call-done = f32[3,365,512]{2,1,0:T(8,128)} async-done(((f32[3,365,512]{2,1,0:T(8,128)}), f32[3,365,512]{2,1,0:T(8,128)}) %all-reduce.6.cloned.1.call-update) | async-done | bytes 2242576 | tf_op jit(solution)/shard_map/psum | solution.py:94
  323.0 2.0 broadcast_divide_fusion
  325.0 2.1 reshape.88
  327.1 3.8 reduce_sum.35
  330.9 71.1 %all-reduce.8.cloned.1.call-done = f32[3,365,128]{2,1,0:T(8,128)} async-done(((f32[3,365,128]{2,1,0:T(8,128)}), f32[3,365,128]{2,1,0:T(8,128)}) %all-reduce.8.cloned.1.call-update) | async-done | bytes 560656 | tf_op jit(solution)/shard_map/psum | solution.py:98
  (45 shorter events, 25.9 us)
Async XLA Ops:
  7.2 5.1 %copy-start = (bf16[2560,512]{1,0:T(8,128)(2,1)S(1)}, bf16[2560,512]{1,0:T(8,128)(2,1)}, u32[]{:S(2)}) copy-start(bf16[2560,512]{1,0:T(8,128)(2,1)} %param.6) | copy-start | bytes 7864324
  7.2 154.8 %all-reduce.4.cloned.1.call-start = ((), (), s32[]{:S(2)}) async-start(), calls=%async_computation | async-start | bytes 5242880 | tf_op jit(solution)/shard_map/psum | solution.py:88
  44.9 278.1 %all-reduce.6.cloned.1.call-start = ((), (), s32[]{:S(2)}) async-start(), calls=%async_computation.1 | async-start | bytes 4521984 | tf_op jit(solution)/shard_map/psum | solution.py:94
  191.4 6.8 %collective-permute-start = (bf16[2,15,512]{2,1,0:T(8,128)(2,1)S(1)}, bf16[2,15,512]{2,1,0:T(8,128)(2,1)S(1)}, u32[]{:S(2)}, u32[]{:S(2)}) collective-permute-start(bf16[2,15,512]{2,1,0:T(8,128)(2,1)S(1)} %get-tuple-element.222), channel_id=1, source_target_pairs={{0,1},{1,2},{2,3},{4,5},{5,6},{6,7},{8,9},{9,10},{10,11},{12,13},{... | collective-permute-start | bytes 92168 | tf_op jit(solution)/shard_map/ppermute | solution.py:19
  196.0 5.2 %collective-permute-start.1 = (bf16[2,15,512]{2,1,0:T(8,128)(2,1)S(1)}, bf16[2,15,512]{2,1,0:T(8,128)(2,1)S(1)}, u32[]{:S(2)}, u32[]{:S(2)}) collective-permute-start(bf16[2,15,512]{2,1,0:T(8,128)(2,1)S(1)} %get-tuple-element.221), channel_id=1, source_target_pairs={{1,0},{2,1},{3,2},{5,4},{6,5},{7,6},{9,8},{10,9},{11,10},{13,12},{... | collective-permute-start | bytes 92168 | tf_op jit(solution)/shard_map/ppermute | solution.py:20
  271.2 130.7 %all-reduce.8.cloned.1.call-start = ((), (), s32[]{:S(2)}) async-start(), calls=%async_computation.2 | async-start | bytes 1130496 | tf_op jit(solution)/shard_map/psum | solution.py:98
  325.0 5.9 %copy-start.1 = (f32[3,365,512]{2,1,0:T(8,128)}, f32[3,365,512]{2,1,0:T(8,128)S(1)}, u32[]{:S(2)}) copy-start(f32[3,365,512]{2,1,0:T(8,128)S(1)} %broadcast_divide_fusion) | copy-start | bytes 6727684
Sparse Core Ops, SparseCore 0:
  45.0 116.8 all-reduce.3
  271.4 51.5 all-reduce.5
  331.0 70.9 all-reduce.7
where the time goes:
time: 415 us; the launch traced here: 410 us
  waiting for transfers between devices  238 us (57%)
  local copies, waits for them, and re-layouts  66.7 us (16%)
  other arithmetic  53.5 us (13%)
  matrix products  26.4 us (6%)
  between operations  13.8 us (3%)
  starting transfers between devices  6.84 us (2%)
  blocking collectives  5.12 us (1%)
    psum x1, waiting for transfers between devices, local(): zonal_mean = lax.psum(partial_value, 'cells') / lon_total  117 us
    psum x1, waiting for transfers between devices, local(): zonal_climate = lax.psum(zonal_part, 'cells') / lon_total  71.1 us
    psum x1, waiting for transfers between devices, local(): totals, tallies = lax.psum((totals, tallies), 'tm')  46.6 us
    reduce_sum x1, other arithmetic, local(): jnp.sum(stacked.reshape(2, frames, longitudes, LAT), axis=2, dtype=jnp.fl...  29.8 us
    concatenate x1, local copies, waits for them, and re-layouts, extended(): shard = jnp.concatenate([before, shard, after], axis=dim)  27.2 us
    dot_general x5, matrix products, advance(): jnp.einsum('dt,stc->sdc', inside.astype(jnp.bfloat16), products, preferre...  19.4 us
    another operation x2, local copies, waits for them, and re-layouts, local(): jnp.tile(zonal_mean, (1, 1, longitudes))  17.8 us
    convert_element_type x1, other arithmetic, local(): (stacked.astype(jnp.float32) - jnp.tile(zonal_mean, (1, 1, longitudes)))....  8.92 us
  transfers between devices with their start and end apart: 5, of which 4 were waited for; matrix products, arithmetic and copies ran while one was open for 0% of the time, Pallas kernels for 0%

commit v1 on v0

v1 whole, which is shorter than its diff:
```python
import functools

import jax
import jax.numpy as jnp
import numpy as np
from jax import lax
from jax.experimental import pallas as pl
from jax.experimental.pallas import tpu as pltpu
from jax.sharding import PartitionSpec as P

LAT = 128
HALF = 15
WIN = 7
DAYS = 365
DROWS = 384
EDGE = 16
TILE = 128
SLAB = TILE + 2 * EDGE
LIMIT = 48 * 1024 * 1024
MESH = pl.DeviceIdType.MESH
F32 = jnp.float32
BF16 = jnp.bfloat16


def vmem():
    return pl.BlockSpec(memory_space=pltpu.VMEM)


def taps_matrix():
    k = np.arange(SLAB)[None, :] - np.arange(TILE)[:, None] - EDGE
    x = np.where(k == 0, 1.0, k).astype(np.float64)
    response = (np.sin(np.pi * x) - np.sin(0.25 * np.pi * x)) / (np.pi * x)
    smoother = np.sin(np.pi * x / (HALF + 1)) / (np.pi * x / (HALF + 1))
    w = np.where(k == 0, 0.75, response * smoother)
    return jnp.asarray(np.where(np.abs(k) <= HALF, w, 0.0).astype(np.float32)).astype(BF16)


def lane_sum(block):
    total = block[:, :LAT].astype(F32)
    for start in range(LAT, block.shape[1], LAT):
        total = total + block[:, start : start + LAT].astype(F32)
    return total


def mean_kernel(n, rows_f, lon_total, geo, mer, halo, mean, part, inbox, ssem, rsem, gssem, grsem):
    me = lax.axis_index("cells")
    frames = geo.shape[0]
    share = part.shape[0] // n
    barrier = pltpu.get_barrier_semaphore()
    for k in range(1, n):
        pl.semaphore_signal(barrier, inc=1, device_id={"cells": lax.rem(me + k, n)}, device_id_type=MESH)

    for f, ref in enumerate((geo, mer)):

        @pl.loop(0, frames // 256)
        def _(i):
            r = pl.multiple_of(i * 256, 256)
            part[pl.ds(f * rows_f + r, 256), :] = lane_sum(ref[pl.ds(r, 256), :]).astype(BF16)

        base = f * rows_f + frames
        part[base : base + 2 * EDGE, :] = lane_sum(halo[f]).astype(BF16)
        rest = rows_f - frames - 2 * EDGE
        if rest:
            part[base + 2 * EDGE : base + 2 * EDGE + rest, :] = jnp.zeros((rest, LAT), BF16)

    pl.semaphore_wait(barrier, n - 1)
    copies = []
    for k in range(1, n):
        peer = lax.rem(me + k, n)
        copy = pltpu.make_async_remote_copy(
            src_ref=part.at[pl.ds(pl.multiple_of(peer * share, 16), share)],
            dst_ref=inbox.at[k - 1],
            send_sem=ssem.at[k - 1],
            recv_sem=rsem.at[k - 1],
            device_id={"cells": peer},
            device_id_type=MESH,
        )
        copy.start()
        copies.append(copy)
    mine = pl.ds(pl.multiple_of(me * share, 16), share)
    total = part[mine, :].astype(F32)
    for k in range(1, n):
        copies[k - 1].wait_recv()
        total = total + inbox[k - 1].astype(F32)
    mean[mine, :] = total / lon_total
    gathers = []
    for k in range(1, n):
        peer = lax.rem(me + k, n)
        copy = pltpu.make_async_remote_copy(
            src_ref=mean.at[mine],
            dst_ref=mean.at[mine],
            send_sem=gssem.at[k - 1],
            recv_sem=grsem.at[k - 1],
            device_id={"cells": peer},
            device_id_type=MESH,
        )
        copy.start()
        gathers.append(copy)
    for k in range(1, n):
        copies[k - 1].wait_send()
        gathers[k - 1].wait_send()
        source = lax.rem(me + n - k, n)
        theirs = mean.at[pl.ds(pl.multiple_of(source * share, 16), share)]
        pltpu.make_async_remote_copy(
            src_ref=theirs,
            dst_ref=theirs,
            send_sem=gssem.at[k - 1],
            recv_sem=grsem.at[k - 1],
            device_id={"cells": source},
            device_id_type=MESH,
        ).wait_recv()


def day_kernel(rows_f, geo, mer, halo, mean, days, taps, raw, padded, products, onehot):
    frames, width = geo.shape
    lons = width // LAT

    def put(field, dst, block, m):
        for j in range(lons):
            cols = slice(field * width + j * LAT, field * width + (j + 1) * LAT)
            padded[dst, cols] = (block[:, j * LAT : (j + 1) * LAT].astype(F32) - m).astype(BF16)

    for f, ref in enumerate((geo, mer)):
        base = f * rows_f + frames
        put(f, slice(0, EDGE), halo[f, :EDGE], mean[base : base + EDGE, :])
        put(f, slice(frames + EDGE, frames + 2 * EDGE), halo[f, EDGE:], mean[base + EDGE : base + 2 * EDGE, :])

        @pl.loop(0, frames // 128)
        def _(i):
            r = pl.multiple_of(i * 128, 128)
            put(f, pl.ds(r + EDGE, 128), ref[pl.ds(r, 128), :], mean[pl.ds(f * rows_f + r, 128), :])

    @pl.loop(0, frames // TILE)
    def _(i):
        r = pl.multiple_of(i * TILE, TILE)
        hit = lax.broadcasted_iota(jnp.int32, (DROWS, TILE), 0) == days[:, pl.ds(r, TILE)]
        onehot[:, pl.ds(r, TILE)] = jnp.where(hit, 1.0, 0.0).astype(BF16)
        for j in range(width // 256):
            lo, hi = j * 256, (j + 1) * 256
            a = jnp.dot(taps[...], padded[pl.ds(r, SLAB), lo:hi], preferred_element_type=F32)
            b = jnp.dot(taps[...], padded[pl.ds(r, SLAB), width + lo : width + hi], preferred_element_type=F32)
            products[pl.ds(r, TILE), lo:hi] = (a * a).astype(BF16)
            products[pl.ds(r, TILE), width + lo : width + hi] = (b * b).astype(BF16)
            products[pl.ds(r, TILE), 2 * width + lo : 2 * width + hi] = (a * b).astype(BF16)

    for s in range(3):

        @pl.loop(0, width // 256)
        def _(j):
            c = pl.multiple_of(j * 256, 256)
            raw[s * DROWS : (s + 1) * DROWS, pl.ds(c, 256)] = jnp.dot(
                onehot[...], products[:, pl.ds(s * width + c, 256)], preferred_element_type=F32
            )


def climate_kernel(
    n, zrows, lon_total, raw, tally, climate, zonal, inbox, own, other, zpart, zbox, sems, zsend, zrecv, gsend, grecv, tsend, trecv
):
    me = lax.axis_index("cells")
    tm = lax.axis_index("tm")
    core = lax.rem(tm, 2)
    partner = tm + 1 - 2 * core
    across = lax.rem(tm + 2, 4)
    half = raw.shape[1] // 2
    share = zrows // n
    barrier = pltpu.get_barrier_semaphore()
    for k in range(1, n):
        pl.semaphore_signal(barrier, inc=1, device_id={"cells": lax.rem(me + k, n)}, device_id_type=MESH)
    for k in range(1, 4):
        pl.semaphore_signal(barrier, inc=1, device_id={"tm": lax.rem(tm + k, 4)}, device_id_type=MESH)
    pl.semaphore_wait(barrier, n + 2)

    mine = pl.ds(pl.multiple_of(core * half, 128), half)
    theirs = pl.ds(pl.multiple_of((1 - core) * half, 128), half)
    first = pltpu.make_async_remote_copy(
        src_ref=raw.at[:, theirs], dst_ref=inbox, send_sem=sems.at[0], recv_sem=sems.at[1],
        device_id={"tm": partner}, device_id_type=MESH,
    )
    first.start()
    first.wait()
    own[...] = (raw[:, mine] + inbox[...]).astype(BF16)
    second = pltpu.make_async_remote_copy(
        src_ref=own, dst_ref=other, send_sem=sems.at[2], recv_sem=sems.at[3],
        device_id={"tm": across}, device_id_type=MESH,
    )
    second.start()
    d = lax.broadcasted_iota(jnp.int32, (DROWS, DROWS), 0)
    e = lax.broadcasted_iota(jnp.int32, (DROWS, DROWS), 1)
    gap = jnp.abs(d - e)
    inside = ((gap <= WIN) | (gap >= DAYS - WIN)) & (e < DAYS)
    window = jnp.where(inside, 1.0, 0.0).astype(BF16)
    for s in range(3):
        rows = slice(s * DROWS, (s + 1) * DROWS)
        inbox[rows, :] = jnp.dot(window, own[rows, :], preferred_element_type=F32)
    second.wait()
    for s in range(3):
        rows = slice(s * DROWS, (s + 1) * DROWS)
        total = inbox[rows, :] + jnp.dot(window, other[rows, :], preferred_element_type=F32)
        for j in range(half // LAT):
            cols = pl.ds(pl.multiple_of(core * half + j * LAT, 128), LAT)
            climate[rows, cols] = total[:, j * LAT : (j + 1) * LAT] / tally[...]
    third = pltpu.make_async_remote_copy(
        src_ref=climate.at[:, mine], dst_ref=climate.at[:, mine], send_sem=sems.at[4], recv_sem=sems.at[5],
        device_id={"tm": partner}, device_id_type=MESH,
    )
    third.start()
    third.wait_send()
    pltpu.make_async_remote_copy(
        src_ref=climate.at[:, theirs], dst_ref=climate.at[:, theirs], send_sem=sems.at[4], recv_sem=sems.at[5],
        device_id={"tm": partner}, device_id_type=MESH,
    ).wait_recv()

    quarter = climate.shape[0] // 4
    q = pl.multiple_of(tm * quarter, 8)
    zpart[:quarter, :] = lane_sum(climate[pl.ds(q, quarter), :])
    if zrows > quarter:
        zpart[quarter:, :] = jnp.zeros((zrows - quarter, LAT), F32)
    copies = []
    for k in range(1, n):
        peer = lax.rem(me + k, n)
        copy = pltpu.make_async_remote_copy(
            src_ref=zpart.at[pl.ds(pl.multiple_of(peer * share, 8), share)],
            dst_ref=zbox.at[k - 1], send_sem=zsend.at[k - 1], recv_sem=zrecv.at[k - 1],
            device_id={"cells": peer}, device_id_type=MESH,
        )
        copy.start()
        copies.append(copy)
    block = pl.ds(pl.multiple_of(me * share, 8), share)
    total = zpart[block, :]
    for k in range(1, n):
        copies[k - 1].wait_recv()
        total = total + zbox[k - 1]
    zonal[tm, block, :] = total / lon_total
    gathers = []
    for k in range(1, n):
        copy = pltpu.make_async_remote_copy(
            src_ref=zonal.at[tm, block], dst_ref=zonal.at[tm, block],
            send_sem=gsend.at[k - 1], recv_sem=grecv.at[k - 1],
            device_id={"cells": lax.rem(me + k, n)}, device_id_type=MESH,
        )
        copy.start()
        gathers.append(copy)
    for k in range(1, n):
        copies[k - 1].wait_send()
        gathers[k - 1].wait_send()
        source = lax.rem(me + n - k, n)
        there = zonal.at[tm, pl.ds(pl.multiple_of(source * share, 8), share)]
        pltpu.make_async_remote_copy(
            src_ref=there, dst_ref=there, send_sem=gsend.at[k - 1], recv_sem=grecv.at[k - 1],
            device_id={"cells": source}, device_id_type=MESH,
        ).wait_recv()
    spreads = []
    for k in range(1, 4):
        copy = pltpu.make_async_remote_copy(
            src_ref=zonal.at[tm], dst_ref=zonal.at[tm],
            send_sem=tsend.at[k - 1], recv_sem=trecv.at[k - 1],
            device_id={"tm": lax.rem(tm + k, 4)}, device_id_type=MESH,
        )
        copy.start()
        spreads.append(copy)
    for k in range(1, 4):
        spreads[k - 1].wait_send()
        source = lax.rem(tm + 4 - k, 4)
        pltpu.make_async_remote_copy(
            src_ref=zonal.at[source], dst_ref=zonal.at[source],
            send_sem=tsend.at[k - 1], recv_sem=trecv.at[k - 1],
            device_id={"tm": source}, device_id_type=MESH,
        ).wait_recv()


def local(geopotential, meridional, day_index):
    frames, width = geopotential.shape
    n = lax.axis_size("cells")
    size = lax.axis_size("tm")
    lon_total = width // LAT * n
    step = 8 * n
    rows_f = -(-(frames + 2 * EDGE) // step) * step
    share = 2 * rows_f // n

    up = [(i, i + 1) for i in range(size - 1)]
    down = [(j, i) for i, j in up]
    before = lax.ppermute(jnp.stack([geopotential[-EDGE:], meridional[-EDGE:]]), "tm", up)
    after = lax.ppermute(jnp.stack([geopotential[:EDGE], meridional[:EDGE]]), "tm", down)
    halo = jnp.concatenate([before, after], axis=1)

    counts = jnp.sum((jnp.arange(DAYS)[:, None] == day_index[None, :]).astype(F32), axis=1)
    counts = lax.psum(counts, "tm")
    gap = jnp.abs(jnp.arange(DROWS)[:, None] - jnp.arange(DAYS)[None, :])
    near = (gap <= WIN) | (gap >= DAYS - WIN)
    tallies = jnp.sum(jnp.where(near, counts[None, :], 0.0), axis=1)
    tally = jnp.broadcast_to(jnp.where(jnp.arange(DROWS) < DAYS, tallies, 1.0)[:, None], (DROWS, LAT))

    dma = pltpu.SemaphoreType.DMA
    mean = pl.pallas_call(
        functools.partial(mean_kernel, n, rows_f, float(lon_total)),
        out_shape=jax.ShapeDtypeStruct((2 * rows_f, LAT), F32),
        in_specs=[vmem()] * 3,
        out_specs=vmem(),
        scratch_shapes=[
            pltpu.VMEM((2 * rows_f, LAT), BF16),
            pltpu.VMEM((n - 1, share, LAT), BF16),
            dma((n - 1,)), dma((n - 1,)), dma((n - 1,)), dma((n - 1,)),
        ],
        compiler_params=pltpu.CompilerParams(collective_id=0, has_side_effects=True, vmem_limit_bytes=LIMIT),
    )(geopotential, meridional, halo)

    raw = pl.pallas_call(
        functools.partial(day_kernel, rows_f),
        out_shape=jax.ShapeDtypeStruct((3 * DROWS, width), F32),
        in_specs=[vmem()] * 6,
        out_specs=vmem(),
        scratch_shapes=[
            pltpu.VMEM((frames + 2 * EDGE, 2 * width), BF16),
            pltpu.VMEM((frames, 3 * width), BF16),
            pltpu.VMEM((DROWS, frames), BF16),
        ],
        compiler_params=pltpu.CompilerParams(vmem_limit_bytes=LIMIT),
    )(geopotential, meridional, halo, mean, day_index.reshape(1, frames), taps_matrix())

    quarter = 3 * DROWS // 4
    zshare = -(-quarter // (8 * n)) * 8
    zrows = n * zshare
    climate, zonal = pl.pallas_call(
        functools.partial(climate_kernel, n, zrows, float(lon_total)),
        out_shape=(
            jax.ShapeDtypeStruct((3 * DROWS, width), F32),
            jax.ShapeDtypeStruct((4, zrows, LAT), F32),
        ),
        in_specs=[vmem()] * 2,
        out_specs=(vmem(), vmem()),
        scratch_shapes=[
            pltpu.VMEM((3 * DROWS, width // 2), F32),
            pltpu.VMEM((3 * DROWS, width // 2), BF16),
            pltpu.VMEM((3 * DROWS, width // 2), BF16),
            pltpu.VMEM((zrows, LAT), F32),
            pltpu.VMEM((n - 1, zshare, LAT), F32),
            dma((6,)),
            dma((n - 1,)), dma((n - 1,)), dma((n - 1,)), dma((n - 1,)),
            dma((3,)), dma((3,)),
        ],
        compiler_params=pltpu.CompilerParams(collective_id=1, has_side_effects=True, vmem_limit_bytes=LIMIT),
    )(raw, tally)
    climate = climate.reshape(3, DROWS, width)[:, :DAYS]
    zonal = zonal[:, :quarter].reshape(3, DROWS, LAT)[:, :DAYS]
    return (climate, zonal)


def solution(mesh):
    return jax.shard_map(
        local,
        mesh=mesh,
        in_specs=(P("tm", "cells"), P("tm", "cells"), P("tm")),
        out_specs=(P(None, None, "cells"), P()),
        check_vma=False,
    )
```

time: 415 us -> 182 us (0.44); the launches traced: 410 us -> 182 us
  waiting for transfers between devices: 238 us -> 0.01 us
  Pallas kernels: 0 us -> 160 us
  local copies, waits for them, and re-layouts: 66.7 us -> 7.54 us
  other arithmetic: 53.5 us -> 1.32 us
  matrix products: 26.4 us -> 0 us
  between operations: 13.8 us -> 0.74 us
    psum x3 -> x0, waiting for transfers between devices: 235 us -> none  [the longest x1 117 us: local(): zonal_mean = lax.psum(partial_value, 'cells') / lon_total]
    pallas_call x0 -> x3, Pallas kernels: none -> 160 us  [the longest x1 83.6 us: local(): pl.pallas_call(functools.partial(mean_kernel, n, rows_f, float(lon_total)...]
    reduce_sum x7 -> x2, other arithmetic: 36.8 us -> 1.3 us  [the longest x1 1.17 us: local(): jnp.sum((jnp.arange(DAYS)[:, None] == day_index[None, :]).astype(F32), ax...]
    another operation x9 -> x1, local copies, waits for them, and re-layouts: 32.7 us -> 0.78 us  [local(): jnp.stack([geopotential[:EDGE], meridional[:EDGE]])]
    concatenate x1, local copies, waits for them, and re-layouts: 27.2 us -> 0.01 us  [local(): halo = jnp.concatenate([before, after], axis=1)]
    dot_general x10 -> x0, matrix products: 26.4 us -> none  [the longest x5 19.4 us: advance(): jnp.einsum('dt,stc->sdc', inside.astype(jnp.bfloat16), products, preferre...]
    convert_element_type x1 -> x0, other arithmetic: 8.92 us -> none  [local(): (stacked.astype(jnp.float32) - jnp.tile(zonal_mean, (1, 1, longitudes)))....]
    div x3 -> x0, other arithmetic: 5.76 us -> none  [the longest x1 1.95 us: local(): climate = totals / tallies[None, :, None]]
  transfers between devices with their start and end apart: 5 -> 2, of which waited for: 4 -> 0; matrix products, arithmetic and copies ran while one was open for 0% -> 1% of each run, Pallas kernels for 0% -> 0%
where the time goes in v1:
time: 182 us
  Pallas kernels  160 us (88%)
  local copies, waits for them, and re-layouts  7.54 us (4%)
  starting transfers between devices  6.46 us (4%)
  blocking collectives  5.51 us (3%)
    pallas_call x1, Pallas kernels, local(): pl.pallas_call(functools.partial(mean_kernel, n, rows_f, float(lon_total)...  83.6 us
    pallas_call x1, Pallas kernels, local(): pl.pallas_call(functools.partial(climate_kernel, n, zrows, float(lon_tota...  63.1 us
    pallas_call x1, Pallas kernels, local(): pl.pallas_call(functools.partial(day_kernel, rows_f), out_shape=jax.Shape...  13.4 us
    psum x1, blocking collectives, local(): counts = lax.psum(counts, 'tm')  5.51 us
    ppermute x1, starting transfers between devices, local(): lax.ppermute(jnp.stack([geopotential[-EDGE:], meridional[-EDGE:]]), 'tm',...  4.54 us
  transfers between devices with their start and end apart: 2, of which 0 were waited for; matrix products, arithmetic and copies ran while one was open for 1% of the time, Pallas kernels for 0%

profile of v1, /device:TPU:1, one launch (start us, length us, event | category | flops | bytes accessed | tf_op | source)
XLA Modules:
  0.0 181.7 jit_solution(7224943662594528644)
XLA Ops:
  0.6 0.8 slice_bitcast_fusion
  1.4 4.5 %collective-permute-start = (bf16[2,16,512]{2,1,0:T(8,128)(2,1)S(1)}, bf16[2,16,512]{2,1,0:T(8,128)(2,1)S(1)}, u32[]{:S(2)}, u32[]{:S(2)}) collective-permute-start(bf16[2,16,512]{2,1,0:T(8,128)(2,1)S(1)} %pad_maximum_fusion), channel_id=1, source_target_pairs={{0,1},{1,2},{2,3},{4,5},{5,6},{6,7},{8,9},{9,10},{10,11},{12,13},{... | collective-permute-start | bytes 98312 | tf_op jit(solution)/shard_map/ppermute | solution.py:282
  6.0 1.9 %collective-permute-start.1 = (bf16[2,16,512]{2,1,0:T(8,128)(2,1)S(1)}, bf16[2,16,512]{2,1,0:T(8,128)(2,1)S(1)}, u32[]{:S(2)}, u32[]{:S(2)}) collective-permute-start(bf16[2,16,512]{2,1,0:T(8,128)(2,1)S(1)} %pad_maximum_fusion.1), channel_id=1, source_target_pairs={{1,0},{2,1},{3,2},{5,4},{6,5},{7,6},{9,8},{10,9},{11,10},{13,12},{... | collective-permute-start | bytes 98312 | tf_op jit(solution)/shard_map/ppermute | solution.py:283
  7.9 1.2 convert_reduce_fusion
  9.1 5.5 %psum.7 = f32[365]{0:T(512)S(1)} all-reduce(f32[365]{0:T(512)S(1)} %convert_reduce_fusion), channel_id=1, replica_groups=mesh['cells'=8,'tm'=4] {'tm'}, use_global_device_ids=true, to_apply=%region_1.0 | all-reduce | flops 365 | bytes 2920 | tf_op jit(solution)/shard_map/psum | solution.py:287
  14.6 0.1 select_reduce_fusion
  14.7 0.7 reshape.22.days
  15.4 0.0 collective-permute-done
  15.5 0.0 collective-permute-done.1
  15.5 0.0 copy-start
  15.5 1.7 copy-done
  17.2 0.0 copy-start.1
  17.2 1.7 copy-done.1
  19.0 0.0 copy-start.2
  19.0 83.6 %shard_map.59.mean = f32[5248,128]{1,0:T(8,128)} custom-call(bf16[2560,512]{1,0:T(8,128)(2,1)S(1)} %copy-done, bf16[2560,512]{1,0:T(8,128)(2,1)S(1)} %copy-done.1, bf16[2,32,512]{2,1,0:T(8,128)(2,1)S(1)} %constant_dynamic-update-slice_fusion.halo), custom_call_target="tpu_custom_call" | custom-call | tf_op jit(solution)/shard_map/pallas_call | solution.py:294
  102.6 0.0 copy-done.2
  102.6 13.4 %shard_map.60.raw = f32[1152,512]{1,0:T(8,128)S(1)} custom-call(bf16[2560,512]{1,0:T(8,128)(2,1)S(1)} %copy-done, bf16[2560,512]{1,0:T(8,128)(2,1)} %mer.3, bf16[2,32,512]{2,1,0:T(8,128)(2,1)S(1)} %constant_dynamic-update-slice_fusion.halo, f32[5248,128]{1,0:T(8,128)} %shard_map.59.mean, s32[1,2560]{1,0:T(1,128)S(1)} %reshape.22.days, ...), custom_call_target="tpu_custom_call" | custom-call | tf_op jit(solution)/shard_map/pallas_call | solution.py:307
  116.0 0.1 broadcast_in_dim.30.tally
  116.1 63.1 %shard_map.61 = (f32[1152,512]{1,0:T(8,128)S(1)}, f32[4,320,128]{2,1,0:T(8,128)S(1)}) custom-call(f32[1152,512]{1,0:T(8,128)S(1)} %shard_map.60.raw, f32[384,128]{1,0:T(8,128)S(1)} %broadcast_in_dim.30.tally), custom_call_target="tpu_custom_call" | custom-call | tf_op jit(solution)/shard_map/pallas_call | solution.py:323
  179.2 1.6 slice.28
  180.8 0.8 slice.29
  (6 shorter events, 0.1 us)
Async XLA Ops:
  1.4 14.0 %collective-permute-start = (bf16[2,16,512]{2,1,0:T(8,128)(2,1)S(1)}, bf16[2,16,512]{2,1,0:T(8,128)(2,1)S(1)}, u32[]{:S(2)}, u32[]{:S(2)}) collective-permute-start(bf16[2,16,512]{2,1,0:T(8,128)(2,1)S(1)} %pad_maximum_fusion), channel_id=1, source_target_pairs={{0,1},{1,2},{2,3},{4,5},{5,6},{6,7},{8,9},{9,10},{10,11},{12,13},{... | collective-permute-start | bytes 98312 | tf_op jit(solution)/shard_map/ppermute | solution.py:282
  6.0 9.5 %collective-permute-start.1 = (bf16[2,16,512]{2,1,0:T(8,128)(2,1)S(1)}, bf16[2,16,512]{2,1,0:T(8,128)(2,1)S(1)}, u32[]{:S(2)}, u32[]{:S(2)}) collective-permute-start(bf16[2,16,512]{2,1,0:T(8,128)(2,1)S(1)} %pad_maximum_fusion.1), channel_id=1, source_target_pairs={{1,0},{2,1},{3,2},{5,4},{6,5},{7,6},{9,8},{10,9},{11,10},{13,12},{... | collective-permute-start | bytes 98312 | tf_op jit(solution)/shard_map/ppermute | solution.py:283
  15.5 1.7 copy-start
  17.2 1.7 copy-start.1
  19.0 83.6 %copy-start.2 = (bf16[128,160]{1,0:T(8,128)(2,1)S(1)}, bf16[128,160]{1,0:T(8,128)(2,1)}, u32[]{:S(2)}) copy-start(bf16[128,160]{1,0:T(8,128)(2,1)} %constant.13.taps) | copy-start | bytes 122884

commit v2 on v1

--- a/solution.py
+++ b/solution.py
@@ -42,13 +42,37 @@
     return total
 
 
-def mean_kernel(n, rows_f, lon_total, geo, mer, halo, mean, part, inbox, ssem, rsem, gssem, grsem):
+def mean_kernel(
+    n, rows_f, lon_total, geo, mer, mean, halo, part, inbox, hsem, ssem, rsem, gssem, grsem, fssem, frsem
+):
     me = lax.axis_index("cells")
+    tm = lax.axis_index("tm")
+    lo = lax.rem(me, 2)
+    partner = me + 1 - 2 * lo
     frames = geo.shape[0]
     share = part.shape[0] // n
+    right, left = lax.rem(tm + 1, 4), lax.rem(tm + 3, 4)
     barrier = pltpu.get_barrier_semaphore()
     for k in range(1, n):
         pl.semaphore_signal(barrier, inc=1, device_id={"cells": lax.rem(me + k, n)}, device_id_type=MESH)
+    for peer in (right, left):
+        pl.semaphore_signal(barrier, inc=1, device_id={"tm": peer}, device_id_type=MESH)
+    pl.semaphore_wait(barrier, n + 1)
+
+    edges = []
+    for f, ref in enumerate((geo, mer)):
+        for side, (peer, start) in enumerate(((right, frames - EDGE), (left, 0))):
+            slot = 2 * f + side
+            copy = pltpu.make_async_remote_copy(
+                src_ref=ref.at[start : start + EDGE],
+                dst_ref=halo.at[f, side * EDGE : (side + 1) * EDGE],
+                send_sem=hsem.at[slot],
+                recv_sem=hsem.at[4 + slot],
+                device_id={"tm": peer},
+                device_id_type=MESH,
+            )
+            copy.start()
+            edges.append(copy)
 
     for f, ref in enumerate((geo, mer)):
 
@@ -57,13 +81,19 @@
             r = pl.multiple_of(i * 256, 256)
             part[pl.ds(f * rows_f + r, 256), :] = lane_sum(ref[pl.ds(r, 256), :]).astype(BF16)
 
+    for copy in edges:
+        copy.wait()
+    for f in range(2):
         base = f * rows_f + frames
+        for side, inner in enumerate((tm > 0, tm < 3)):
+            keep = jnp.where(inner, 1.0, 0.0).astype(F32)
+            dst = slice(side * EDGE, (side + 1) * EDGE)
+            halo[f, dst] = (halo[f, dst].astype(F32) * keep).astype(BF16)
         part[base : base + 2 * EDGE, :] = lane_sum(halo[f]).astype(BF16)
         rest = rows_f - frames - 2 * EDGE
         if rest:
             part[base + 2 * EDGE : base + 2 * EDGE + rest, :] = jnp.zeros((rest, LAT), BF16)
 
-    pl.semaphore_wait(barrier, n - 1)
     copies = []
     for k in range(1, n):
         peer = lax.rem(me + k, n)
@@ -83,35 +113,36 @@
         copies[k - 1].wait_recv()
         total = total + inbox[k - 1].astype(F32)
     mean[mine, :] = total / lon_total
+
+    def spread(source, peer, send_sem, recv_sem):
+        rows = mean.at[pl.ds(pl.multiple_of(source * share, 16), share)]
+        return pltpu.make_async_remote_copy(
+            src_ref=rows, dst_ref=rows, send_sem=send_sem, recv_sem=recv_sem,
+            device_id={"cells": peer}, device_id_type=MESH,
+        )
+
+    m = n // 2
+    passes = [spread(me, partner, fssem.at[0], frsem.at[0])]
+    passes[0].start()
     gathers = []
-    for k in range(1, n):
-        peer = lax.rem(me + k, n)
-        copy = pltpu.make_async_remote_copy(
-            src_ref=mean.at[mine],
-            dst_ref=mean.at[mine],
-            send_sem=gssem.at[k - 1],
-            recv_sem=grsem.at[k - 1],
-            device_id={"cells": peer},
-            device_id_type=MESH,
-        )
+    for k in range(1, m):
+        copy = spread(me, lax.rem(me + 2 * k, n), gssem.at[k - 1], grsem.at[k - 1])
         copy.start()
         gathers.append(copy)
-    for k in range(1, n):
-        copies[k - 1].wait_send()
-        gathers[k - 1].wait_send()
-        source = lax.rem(me + n - k, n)
-        theirs = mean.at[pl.ds(pl.multiple_of(source * share, 16), share)]
-        pltpu.make_async_remote_copy(
-            src_ref=theirs,
-            dst_ref=theirs,
-            send_sem=gssem.at[k - 1],
-            recv_sem=grsem.at[k - 1],
-            device_id={"cells": source},
-            device_id_type=MESH,
-        ).wait_recv()
-
-
-def day_kernel(rows_f, geo, mer, halo, mean, days, taps, raw, padded, products, onehot):
+    for k in range(1, m):
+        source = lax.rem(me + n - 2 * k, n)
+        spread(source, source, gssem.at[k - 1], grsem.at[k - 1]).wait_recv()
+        copy = spread(source, partner, fssem.at[k], frsem.at[k])
+        copy.start()
+        passes.append(copy)
+    for k in range(m):
+        source = lax.rem(partner + n - 2 * k, n)
+        spread(source, partner, fssem.at[k], frsem.at[k]).wait_recv()
+    for copy in copies + gathers + passes:
+        copy.wait_send()
+
+
+def day_kernel(rows_f, geo, mer, halo, mean, days, taps, raw, counts, padded, products, onehot):
     frames, width = geo.shape
     lons = width // LAT
 
@@ -143,6 +174,9 @@
             products[pl.ds(r, TILE), width + lo : width + hi] = (b * b).astype(BF16)
             products[pl.ds(r, TILE), 2 * width + lo : 2 * width + hi] = (a * b).astype(BF16)
 
+    counts[...] = lax.dot_general(
+        jnp.ones((8, frames), BF16), onehot[...], (((1,), (1,)), ((), ())), preferred_element_type=F32
+    )
     for s in range(3):
 
         @pl.loop(0, width // 256)
@@ -154,7 +188,8 @@
 
 
 def climate_kernel(
-    n, zrows, lon_total, raw, tally, climate, zonal, inbox, own, other, zpart, zbox, sems, zsend, zrecv, gsend, grecv, tsend, trecv
+    n, zrows, lon_total, raw, counts, climate, zonal, inbox, own, other, cbox, zhalf, zother, zpart, zbox,
+    fsem, ssem, tsem, csem, xsem, zsend, zrecv, gsend, grecv, tsend, trecv,
 ):
     me = lax.axis_index("cells")
     tm = lax.axis_index("tm")
@@ -172,49 +207,68 @@
 
     mine = pl.ds(pl.multiple_of(core * half, 128), half)
     theirs = pl.ds(pl.multiple_of((1 - core) * half, 128), half)
-    first = pltpu.make_async_remote_copy(
-        src_ref=raw.at[:, theirs], dst_ref=inbox, send_sem=sems.at[0], recv_sem=sems.at[1],
-        device_id={"tm": partner}, device_id_type=MESH,
-    )
-    first.start()
-    first.wait()
-    own[...] = (raw[:, mine] + inbox[...]).astype(BF16)
-    second = pltpu.make_async_remote_copy(
-        src_ref=own, dst_ref=other, send_sem=sems.at[2], recv_sem=sems.at[3],
-        device_id={"tm": across}, device_id_type=MESH,
-    )
-    second.start()
+    parts = [slice(s * DROWS, (s + 1) * DROWS) for s in range(3)]
+    first, second, third, tell = [], [], [], []
+    for s, rows in enumerate(parts):
+        first.append(pltpu.make_async_remote_copy(
+            src_ref=raw.at[rows, theirs], dst_ref=inbox.at[rows], send_sem=fsem.at[s], recv_sem=fsem.at[3 + s],
+            device_id={"tm": partner}, device_id_type=MESH,
+        ))
+        first[s].start()
+    for k in range(1, 4):
+        tell.append(pltpu.make_async_remote_copy(
+            src_ref=counts, dst_ref=cbox.at[k - 1], send_sem=csem.at[k - 1], recv_sem=csem.at[2 + k],
+            device_id={"tm": lax.rem(tm + k, 4)}, device_id_type=MESH,
+        ))
+        tell[-1].start()
     d = lax.broadcasted_iota(jnp.int32, (DROWS, DROWS), 0)
     e = lax.broadcasted_iota(jnp.int32, (DROWS, DROWS), 1)
     gap = jnp.abs(d - e)
-    inside = ((gap <= WIN) | (gap >= DAYS - WIN)) & (e < DAYS)
-    window = jnp.where(inside, 1.0, 0.0).astype(BF16)
-    for s in range(3):
-        rows = slice(s * DROWS, (s + 1) * DROWS)
+    inside = jnp.where(((gap <= WIN) | (gap >= DAYS - WIN)) & (e < DAYS), 1.0, 0.0).astype(F32)
+    window = inside.astype(BF16)
+    for s, rows in enumerate(parts):
+        first[s].wait_recv()
+        own[rows, :] = (raw[rows, mine] + inbox[rows, :]).astype(BF16)
+        second.append(pltpu.make_async_remote_copy(
+            src_ref=own.at[rows], dst_ref=other.at[rows], send_sem=ssem.at[s], recv_sem=ssem.at[3 + s],
+            device_id={"tm": across}, device_id_type=MESH,
+        ))
+        second[s].start()
+    for rows in parts:
         inbox[rows, :] = jnp.dot(window, own[rows, :], preferred_element_type=F32)
-    second.wait()
-    for s in range(3):
-        rows = slice(s * DROWS, (s + 1) * DROWS)
+    row = counts[0:1, :]
+    for k in range(3):
+        tell[k].wait()
+        row = row + cbox[k, 0:1, :]
+    tally = jnp.broadcast_to(jnp.sum(inside * row, axis=1, keepdims=True), (DROWS, LAT))
+    for s, rows in enumerate(parts):
+        second[s].wait_recv()
         total = inbox[rows, :] + jnp.dot(window, other[rows, :], preferred_element_type=F32)
+        zonal_sum = jnp.zeros((DROWS, LAT), F32)
         for j in range(half // LAT):
             cols = pl.ds(pl.multiple_of(core * half + j * LAT, 128), LAT)
-            climate[rows, cols] = total[:, j * LAT : (j + 1) * LAT] / tally[...]
-    third = pltpu.make_async_remote_copy(
-        src_ref=climate.at[:, mine], dst_ref=climate.at[:, mine], send_sem=sems.at[4], recv_sem=sems.at[5],
-        device_id={"tm": partner}, device_id_type=MESH,
+            value = total[:, j * LAT : (j + 1) * LAT] / tally
+            climate[rows, cols] = value
+            zonal_sum = zonal_sum + value
+        zhalf[rows, :] = zonal_sum
+        third.append(pltpu.make_async_remote_copy(
+            src_ref=climate.at[rows, mine], dst_ref=climate.at[rows, mine], send_sem=tsem.at[s],
+            recv_sem=tsem.at[3 + s], device_id={"tm": partner}, device_id_type=MESH,
+        ))
+        if s < 2:
+            third[s].start()
+
+    quarter = climate.shape[0] // 4
+    swap = pltpu.make_async_remote_copy(
+        src_ref=zhalf.at[pl.ds(pl.multiple_of(partner * quarter, 8), quarter)], dst_ref=zother,
+        send_sem=xsem.at[0], recv_sem=xsem.at[1], device_id={"tm": partner}, device_id_type=MESH,
     )
-    third.start()
-    third.wait_send()
-    pltpu.make_async_remote_copy(
-        src_ref=climate.at[:, theirs], dst_ref=climate.at[:, theirs], send_sem=sems.at[4], recv_sem=sems.at[5],
-        device_id={"tm": partner}, device_id_type=MESH,
-    ).wait_recv()
-
-    quarter = climate.shape[0] // 4
-    q = pl.multiple_of(tm * quarter, 8)
-    zpart[:quarter, :] = lane_sum(climate[pl.ds(q, quarter), :])
+    swap.start()
+    third[2].start()
     if zrows > quarter:
         zpart[quarter:, :] = jnp.zeros((zrows - quarter, LAT), F32)
+    swap.wait()
+    zpart[:quarter, :] = zhalf[pl.ds(pl.multiple_of(tm * quarter, 8), quarter), :] + zother[...]
     copies = []
     for k in range(1, n):
         peer = lax.rem(me + k, n)
@@ -266,49 +320,50 @@
             send_sem=tsend.at[k - 1], recv_sem=trecv.at[k - 1],
             device_id={"tm": source}, device_id_type=MESH,
         ).wait_recv()
+    for s, rows in enumerate(parts):
+        first[s].wait_send()
+        second[s].wait_send()
+        third[s].wait_send()
+        pltpu.make_async_remote_copy(
+            src_ref=climate.at[rows, theirs], dst_ref=climate.at[rows, theirs], send_sem=tsem.at[s],
+            recv_sem=tsem.at[3 + s], device_id={"tm": partner}, device_id_type=MESH,
+        ).wait_recv()
 
 
 def local(geopotential, meridional, day_index):
     frames, width = geopotential.shape
     n = lax.axis_size("cells")
-    size = lax.axis_size("tm")
     lon_total = width // LAT * n
     step = 8 * n
     rows_f = -(-(frames + 2 * EDGE) // step) * step
     share = 2 * rows_f // n
 
-    up = [(i, i + 1) for i in range(size - 1)]
-    down = [(j, i) for i, j in up]
-    before = lax.ppermute(jnp.stack([geopotential[-EDGE:], meridional[-EDGE:]]), "tm", up)
-    after = lax.ppermute(jnp.stack([geopotential[:EDGE], meridional[:EDGE]]), "tm", down)
-    halo = jnp.concatenate([before, after], axis=1)
-
-    counts = jnp.sum((jnp.arange(DAYS)[:, None] == day_index[None, :]).astype(F32), axis=1)
-    counts = lax.psum(counts, "tm")
-    gap = jnp.abs(jnp.arange(DROWS)[:, None] - jnp.arange(DAYS)[None, :])
-    near = (gap <= WIN) | (gap >= DAYS - WIN)
-    tallies = jnp.sum(jnp.where(near, counts[None, :], 0.0), axis=1)
-    tally = jnp.broadcast_to(jnp.where(jnp.arange(DROWS) < DAYS, tallies, 1.0)[:, None], (DROWS, LAT))
-
     dma = pltpu.SemaphoreType.DMA
-    mean = pl.pallas_call(
+    mean, halo = pl.pallas_call(
         functools.partial(mean_kernel, n, rows_f, float(lon_total)),
-        out_shape=jax.ShapeDtypeStruct((2 * rows_f, LAT), F32),
-        in_specs=[vmem()] * 3,
-        out_specs=vmem(),
+        out_shape=(
+            jax.ShapeDtypeStruct((2 * rows_f, LAT), F32),
+            jax.ShapeDtypeStruct((2, 2 * EDGE, width), BF16),
+        ),
+        in_specs=[vmem()] * 2,
+        out_specs=(vmem(), vmem()),
         scratch_shapes=[
             pltpu.VMEM((2 * rows_f, LAT), BF16),
             pltpu.VMEM((n - 1, share, LAT), BF16),
-            dma((n - 1,)), dma((n - 1,)), dma((n - 1,)), dma((n - 1,)),
+            dma((8,)), dma((n - 1,)), dma((n - 1,)),
+            dma((n // 2 - 1,)), dma((n // 2 - 1,)), dma((n // 2,)), dma((n // 2,)),
         ],
         compiler_params=pltpu.CompilerParams(collective_id=0, has_side_effects=True, vmem_limit_bytes=LIMIT),
-    )(geopotential, meridional, halo)
-
-    raw = pl.pallas_call(
+    )(geopotential, meridional)
+
+    raw, counts = pl.pallas_call(
         functools.partial(day_kernel, rows_f),
-        out_shape=jax.ShapeDtypeStruct((3 * DROWS, width), F32),
+        out_shape=(
+            jax.ShapeDtypeStruct((3 * DROWS, width), F32),
+            jax.ShapeDtypeStruct((8, DROWS), F32),
+        ),
         in_specs=[vmem()] * 6,
-        out_specs=vmem(),
+        out_specs=(vmem(), vmem()),
         scratch_shapes=[
             pltpu.VMEM((frames + 2 * EDGE, 2 * width), BF16),
             pltpu.VMEM((frames, 3 * width), BF16),
@@ -332,14 +387,17 @@
             pltpu.VMEM((3 * DROWS, width // 2), F32),
             pltpu.VMEM((3 * DROWS, width // 2), BF16),
             pltpu.VMEM((3 * DROWS, width // 2), BF16),
+            pltpu.VMEM((3, 8, DROWS), F32),
+            pltpu.VMEM((3 * DROWS, LAT), F32),
+            pltpu.VMEM((quarter, LAT), F32),
             pltpu.VMEM((zrows, LAT), F32),
             pltpu.VMEM((n - 1, zshare, LAT), F32),
-            dma((6,)),
+            dma((6,)), dma((6,)), dma((6,)), dma((6,)), dma((2,)),
             dma((n - 1,)), dma((n - 1,)), dma((n - 1,)), dma((n - 1,)),
             dma((3,)), dma((3,)),
         ],
         compiler_params=pltpu.CompilerParams(collective_id=1, has_side_effects=True, vmem_limit_bytes=LIMIT),
-    )(raw, tally)
+    )(raw, counts)
     climate = climate.reshape(3, DROWS, width)[:, :DAYS]
     zonal = zonal[:, :quarter].reshape(3, DROWS, LAT)[:, :DAYS]
     return (climate, zonal)

time: 182 us -> 147 us (0.81)
  Pallas kernels: 160 us -> 139 us
  starting transfers between devices: 6.46 us -> 0 us
  blocking collectives: 5.51 us -> 0 us
    pallas_call x1, Pallas kernels: 63.1 us -> 47.3 us  [local(): pl.pallas_call(functools.partial(climate_kernel, n, zrows, float(lon_tota...]
    ppermute x2 -> x0, starting transfers between devices: 6.46 us -> none  [the longest x1 4.54 us: local(): lax.ppermute(jnp.stack([geopotential[-EDGE:], meridional[-EDGE:]]), 'tm',...]
    pallas_call x1, Pallas kernels: 83.6 us -> 78 us  [local(): pl.pallas_call(functools.partial(mean_kernel, n, rows_f, float(lon_total)...]
    psum x1 -> x0, blocking collectives: 5.51 us -> none  [local(): counts = lax.psum(counts, 'tm')]
  transfers between devices with their start and end apart: 2 -> 0, of which waited for: 0 -> 0; matrix products, arithmetic and copies ran while one was open for 1% -> 0% of each run, Pallas kernels for 0% -> 0%
where the time goes in v2:
time: 147 us
  Pallas kernels  139 us (95%)
  local copies, waits for them, and re-layouts  6.64 us (5%)
    pallas_call x1, Pallas kernels, local(): pl.pallas_call(functools.partial(mean_kernel, n, rows_f, float(lon_total)...  78 us
    pallas_call x1, Pallas kernels, local(): pl.pallas_call(functools.partial(climate_kernel, n, zrows, float(lon_tota...  47.3 us
    pallas_call x1, Pallas kernels, local(): pl.pallas_call(functools.partial(day_kernel, rows_f), out_shape=(jax.Shap...  14.2 us
    unnamed x6, local copies, waits for them, and re-layouts  3.48 us

profile of v2, /device:TPU:1, one launch (start us, length us, event | category | flops | bytes accessed | tf_op | source)
XLA Modules:
  0.0 146.8 jit_solution(5897510112723192568)
XLA Ops:
  0.6 0.7 reshape.13.days
  1.3 0.0 copy-start
  1.3 1.7 %copy-done = bf16[2560,512]{1,0:T(8,128)(2,1)S(1)} copy-done((bf16[2560,512]{1,0:T(8,128)(2,1)S(1)}, bf16[2560,512]{1,0:T(8,128)(2,1)}, u32[]{:S(2)}) %copy-start) | copy-done | bytes 2621464
  3.1 0.0 copy-start.1
  3.1 1.7 %copy-done.1 = bf16[2560,512]{1,0:T(8,128)(2,1)S(1)} copy-done((bf16[2560,512]{1,0:T(8,128)(2,1)S(1)}, bf16[2560,512]{1,0:T(8,128)(2,1)}, u32[]{:S(2)}) %copy-start.1) | copy-done | bytes 2621464
  4.8 0.0 copy-start.2
  4.8 78.0 %shard_map.59 = (f32[5248,128]{1,0:T(8,128)}, bf16[2,32,512]{2,1,0:T(8,128)(2,1)S(1)}) custom-call(bf16[2560,512]{1,0:T(8,128)(2,1)S(1)} %copy-done, bf16[2560,512]{1,0:T(8,128)(2,1)S(1)} %copy-done.1), custom_call_target="tpu_custom_call" | custom-call | tf_op jit(solution)/shard_map/pallas_call | solution.py:342
  82.9 0.0 copy-done.2
  82.9 14.2 %shard_map.60 = (f32[1152,512]{1,0:T(8,128)S(1)}, f32[8,384]{1,0:T(8,128)S(1)}) custom-call(bf16[2560,512]{1,0:T(8,128)(2,1)S(1)} %copy-done, bf16[2560,512]{1,0:T(8,128)(2,1)} %mer.3, bf16[2,32,512]{2,1,0:T(8,128)(2,1)S(1)} %get-tuple-element.8.halo, f32[5248,128]{1,0:T(8,128)} %get-tuple-element.9.mean, s32[1,2560]{1,0:T(1,128)S(1)} %reshape.13.days, ...), custom_call_target="tpu_custom_call" | custom-call | tf_op jit(solution)/shard_map/pallas_call | solution.py:359
  97.1 47.3 %shard_map.61 = (f32[1152,512]{1,0:T(8,128)S(1)}, f32[4,320,128]{2,1,0:T(8,128)S(1)}) custom-call(f32[1152,512]{1,0:T(8,128)S(1)} %get-tuple-element.10.raw, f32[8,384]{1,0:T(8,128)S(1)} %get-tuple-element.11.counts), custom_call_target="tpu_custom_call" | custom-call | tf_op jit(solution)/shard_map/pallas_call | solution.py:378
  144.3 1.6 %slice.12 = f32[3,365,512]{2,1,0:T(8,128)} slice(f32[3,384,512]{2,1,0:T(8,128)S(1)} %bitcast.2), slice={[0:3], [0:365], [0:512]} | slice | bytes 4485120 | tf_op jit(solution)/shard_map/slice | solution.py:401
  145.9 0.8 slice.13
  (1 shorter events, 0.0 us)
Async XLA Ops:
  1.3 1.7 %copy-start = (bf16[2560,512]{1,0:T(8,128)(2,1)S(1)}, bf16[2560,512]{1,0:T(8,128)(2,1)}, u32[]{:S(2)}) copy-start(bf16[2560,512]{1,0:T(8,128)(2,1)} %geo.3) | copy-start | bytes 7864324
  3.1 1.7 %copy-start.1 = (bf16[2560,512]{1,0:T(8,128)(2,1)S(1)}, bf16[2560,512]{1,0:T(8,128)(2,1)}, u32[]{:S(2)}) copy-start(bf16[2560,512]{1,0:T(8,128)(2,1)} %mer.3) | copy-start | bytes 7864324
  4.8 78.0 %copy-start.2 = (bf16[128,160]{1,0:T(8,128)(2,1)S(1)}, bf16[128,160]{1,0:T(8,128)(2,1)}, u32[]{:S(2)}) copy-start(bf16[128,160]{1,0:T(8,128)(2,1)} %constant.3.taps) | copy-start | bytes 122884

commit v3 on v2

v3 whole, which is shorter than its diff:
```python
import functools

import jax
import jax.numpy as jnp
import numpy as np
from jax import lax
from jax.experimental import pallas as pl
from jax.experimental.pallas import tpu as pltpu
from jax.sharding import PartitionSpec as P

LAT = 128
HALF = 15
WIN = 7
DAYS = 365
DROWS = 384
EDGE = 16
TILE = 128
SLAB = TILE + 2 * EDGE
LIMIT = 48 * 1024 * 1024
MESH = pl.DeviceIdType.MESH
F32 = jnp.float32
BF16 = jnp.bfloat16


def vmem():
    return pl.BlockSpec(memory_space=pltpu.VMEM)


def taps_matrix():
    k = np.arange(SLAB)[None, :] - np.arange(TILE)[:, None] - EDGE
    x = np.where(k == 0, 1.0, k).astype(np.float64)
    response = (np.sin(np.pi * x) - np.sin(0.25 * np.pi * x)) / (np.pi * x)
    smoother = np.sin(np.pi * x / (HALF + 1)) / (np.pi * x / (HALF + 1))
    w = np.where(k == 0, 0.75, response * smoother)
    return jnp.asarray(np.where(np.abs(k) <= HALF, w, 0.0).astype(np.float32)).astype(BF16)


def lane_sum(block):
    total = block[:, :LAT].astype(F32)
    for start in range(LAT, block.shape[1], LAT):
        total = total + block[:, start : start + LAT].astype(F32)
    return total


def eddy_kernel(
    n, lon_total, zrows, pieces, geo_in, mer_in, days, taps, climate, zonal,
    geo, mer, halo, part, mbox, mean, padded, products, onehot, counts, give, keep,
    inbox, own, other, cbox, zhalf, zother, zpart, zbox,
    lsem, hsem, rsend, rrecv, gssem, grsem, fssem, frsem,
    fsem, ssem, tsem, csem, xsem, zsend, zrecv, gsend, grecv, tsend, trecv,
):
    me = lax.axis_index("cells")
    tm = lax.axis_index("tm")
    lo = lax.rem(me, 2)
    mate = me + 1 - 2 * lo
    core = lax.rem(tm, 2)
    partner = tm + 1 - 2 * core
    across = lax.rem(tm + 2, 4)
    frames, width = geo.shape
    lons = width // LAT
    half = width // 2
    count = len(pieces)
    length = frames // count
    share = zrows // n
    m = n // 2
    barrier = pltpu.get_barrier_semaphore()
    for k in range(1, n):
        pl.semaphore_signal(barrier, inc=1, device_id={"cells": lax.rem(me + k, n)}, device_id_type=MESH)
    for k in range(1, 4):
        pl.semaphore_signal(barrier, inc=1, device_id={"tm": lax.rem(tm + k, 4)}, device_id_type=MESH)

    loads = []
    for p in range(count):
        rows = slice(p * length, (p + 1) * length)
        for f, (src, dst) in enumerate(((geo_in, geo), (mer_in, mer))):
            copy = pltpu.make_async_copy(src.at[rows], dst.at[rows], lsem.at[2 * p + f])
            copy.start()
            loads.append(copy)
    pl.semaphore_wait(barrier, n + 2)

    edges = []
    right, left = lax.rem(tm + 1, 4), lax.rem(tm + 3, 4)
    for f, ref in enumerate((geo_in, mer_in)):
        for side, (peer, start) in enumerate(((right, frames - EDGE), (left, 0))):
            slot = 2 * f + side
            copy = pltpu.make_async_remote_copy(
                src_ref=ref.at[start : start + EDGE],
                dst_ref=halo.at[f, side * EDGE : (side + 1) * EDGE],
                send_sem=hsem.at[slot],
                recv_sem=hsem.at[4 + slot],
                device_id={"tm": peer},
                device_id_type=MESH,
            )
            copy.start()
            edges.append(copy)

    sends = []
    scattered = [[] for _ in range(count)]

    def lanes(p):
        base, total_rows = pieces[p]
        loads[2 * p].wait()
        loads[2 * p + 1].wait()
        for f, ref in enumerate((geo, mer)):

            @pl.loop(0, length // 128)
            def _(i):
                r = pl.multiple_of(i * 128, 128)
                part[pl.ds(base + f * length + r, 128), :] = lane_sum(ref[pl.ds(p * length + r, 128), :]).astype(BF16)

        used = 2 * length
        if p == 0:
            for copy in edges:
                copy.wait()
            for f in range(2):
                for side, inner in enumerate((tm > 0, tm < 3)):
                    hold = jnp.where(inner, 1.0, 0.0).astype(F32)
                    dst = slice(side * EDGE, (side + 1) * EDGE)
                    halo[f, dst] = (halo[f, dst].astype(F32) * hold).astype(BF16)
                part[base + used : base + used + 2 * EDGE, :] = lane_sum(halo[f]).astype(BF16)
                used += 2 * EDGE
        if total_rows > used:
            part[base + used : base + total_rows, :] = jnp.zeros((total_rows - used, LAT), BF16)

    def chunk(p, source):
        base, total_rows = pieces[p]
        size = total_rows // n
        return pl.ds(pl.multiple_of(base + source * size, 16), size)

    def scatter(p):
        size = pieces[p][1] // n
        for k in range(1, n):
            peer = lax.rem(me + k, n)
            copy = pltpu.make_async_remote_copy(
                src_ref=part.at[chunk(p, peer)],
                dst_ref=mbox.at[p, k - 1, :size],
                send_sem=rsend.at[p, k - 1],
                recv_sem=rrecv.at[p, k - 1],
                device_id={"cells": peer},
                device_id_type=MESH,
            )
            copy.start()
            scattered[p].append(copy)
            sends.append(copy)

    def spread(p, source, peer, send_sem, recv_sem):
        rows = mean.at[chunk(p, source)]
        return pltpu.make_async_remote_copy(
            src_ref=rows, dst_ref=rows, send_sem=send_sem, recv_sem=recv_sem,
            device_id={"cells": peer}, device_id_type=MESH,
        )

    def reduce(p):
        size = pieces[p][1] // n
        mine = chunk(p, me)
        total = part[mine, :].astype(F32)
        for k in range(1, n):
            scattered[p][k - 1].wait_recv()
            total = total + mbox[p, k - 1, :size].astype(F32)
        mean[mine, :] = total / lon_total
        copy = spread(p, me, mate, fssem.at[p, 0], frsem.at[p, 0])
        copy.start()
        sends.append(copy)
        for k in range(1, m):
            copy = spread(p, me, lax.rem(me + 2 * k, n), gssem.at[p, k - 1], grsem.at[p, k - 1])
            copy.start()
            sends.append(copy)

    def forward(p):
        for k in range(1, m):
            source = lax.rem(me + n - 2 * k, n)
            spread(p, source, source, gssem.at[p, k - 1], grsem.at[p, k - 1]).wait_recv()
            copy = spread(p, source, mate, fssem.at[p, k], frsem.at[p, k])
            copy.start()
            sends.append(copy)

    def settle(p):
        for k in range(m):
            source = lax.rem(mate + n - 2 * k, n)
            spread(p, source, mate, fssem.at[p, k], frsem.at[p, k]).wait_recv()

    def put(field, dst, block, value):
        for j in range(lons):
            cols = slice(field * width + j * LAT, field * width + (j + 1) * LAT)
            padded[dst, cols] = (block[:, j * LAT : (j + 1) * LAT].astype(F32) - value).astype(BF16)

    def anomalies(p):
        base = pieces[p][0]
        for f, ref in enumerate((geo, mer)):
            if p == 0:
                at = base + 2 * length + f * 2 * EDGE
                put(f, slice(0, EDGE), halo[f, :EDGE], mean[at : at + EDGE, :])
                end = frames + EDGE
                put(f, slice(end, end + EDGE), halo[f, EDGE:], mean[at + EDGE : at + 2 * EDGE, :])

            @pl.loop(0, length // 128)
            def _(i):
                r = pl.multiple_of(i * 128, 128)
                dst = pl.ds(pl.multiple_of(p * length + EDGE + r, 16), 128)
                put(f, dst, ref[pl.ds(p * length + r, 128), :], mean[pl.ds(base + f * length + r, 128), :])

    def filtering(p):
        tiles = length // TILE
        start = p * tiles - 1 if p else 0
        stop = (p + 1) * tiles - (0 if p == count - 1 else 1)

        @pl.loop(start, stop)
        def _(i):
            r = pl.multiple_of(i * TILE, TILE)
            for j in range(width // 256):
                a0, a1 = j * 256, (j + 1) * 256
                a = jnp.dot(taps[...], padded[pl.ds(r, SLAB), a0:a1], preferred_element_type=F32)
                b = jnp.dot(taps[...], padded[pl.ds(r, SLAB), width + a0 : width + a1], preferred_element_type=F32)
                products[pl.ds(r, TILE), a0:a1] = (a * a).astype(BF16)
                products[pl.ds(r, TILE), width + a0 : width + a1] = (b * b).astype(BF16)
                products[pl.ds(r, TILE), 2 * width + a0 : 2 * width + a1] = (a * b).astype(BF16)

    tell = []
    for t in range(count + 3):
        if t < count:
            lanes(t)
            scatter(t)
        if 1 <= t <= count:
            if t == 1:

                @pl.loop(0, frames // TILE)
                def _(i):
                    r = pl.multiple_of(i * TILE, TILE)
                    hit = lax.broadcasted_iota(jnp.int32, (DROWS, TILE), 0) == days[:, pl.ds(r, TILE)]
                    onehot[:, pl.ds(r, TILE)] = jnp.where(hit, 1.0, 0.0).astype(BF16)

                counts[...] = lax.dot_general(
                    jnp.ones((8, frames), BF16), onehot[...], (((1,), (1,)), ((), ())), preferred_element_type=F32
                )
                for k in range(1, 4):
                    copy = pltpu.make_async_remote_copy(
                        src_ref=counts, dst_ref=cbox.at[k - 1], send_sem=csem.at[k - 1], recv_sem=csem.at[2 + k],
                        device_id={"tm": lax.rem(tm + k, 4)}, device_id_type=MESH,
                    )
                    copy.start()
                    tell.append(copy)
            reduce(t - 1)
        if 2 <= t <= count + 1:
            forward(t - 2)
        if t >= 3:
            settle(t - 3)
            anomalies(t - 3)
            filtering(t - 3)

    mine = pl.ds(pl.multiple_of(core * half, 128), half)
    theirs = pl.ds(pl.multiple_of((1 - core) * half, 128), half)
    parts = [slice(s * DROWS, (s + 1) * DROWS) for s in range(3)]
    first, second, third = [], [], []
    for s, rows in enumerate(parts):
        cols = pl.ds(pl.multiple_of(s * width + (1 - core) * half, 128), half)
        give[rows, :] = jnp.dot(onehot[...], products[:, cols], preferred_element_type=F32)
        first.append(pltpu.make_async_remote_copy(
            src_ref=give.at[rows], dst_ref=inbox.at[rows], send_sem=fsem.at[s], recv_sem=fsem.at[3 + s],
            device_id={"tm": partner}, device_id_type=MESH,
        ))
        first[s].start()
    for s, rows in enumerate(parts):
        cols = pl.ds(pl.multiple_of(s * width + core * half, 128), half)
        keep[rows, :] = jnp.dot(onehot[...], products[:, cols], preferred_element_type=F32)
        first[s].wait_recv()
        own[rows, :] = (keep[rows, :] + inbox[rows, :]).astype(BF16)
        second.append(pltpu.make_async_remote_copy(
            src_ref=own.at[rows], dst_ref=other.at[rows], send_sem=ssem.at[s], recv_sem=ssem.at[3 + s],
            device_id={"tm": across}, device_id_type=MESH,
        ))
        second[s].start()
    d = lax.broadcasted_iota(jnp.int32, (DROWS, DROWS), 0)
    e = lax.broadcasted_iota(jnp.int32, (DROWS, DROWS), 1)
    gap = jnp.abs(d - e)
    inside = jnp.where(((gap <= WIN) | (gap >= DAYS - WIN)) & (e < DAYS), 1.0, 0.0).astype(F32)
    window = inside.astype(BF16)
    for rows in parts:
        inbox[rows, :] = jnp.dot(window, own[rows, :], preferred_element_type=F32)
    row = counts[0:1, :]
    for k in range(3):
        tell[k].wait()
        row = row + cbox[k, 0:1, :]
    tally = jnp.broadcast_to(jnp.sum(inside * row, axis=1, keepdims=True), (DROWS, LAT))
    for s, rows in enumerate(parts):
        second[s].wait_recv()
        total = inbox[rows, :] + jnp.dot(window, other[rows, :], preferred_element_type=F32)
        zonal_sum = jnp.zeros((DROWS, LAT), F32)
        for j in range(half // LAT):
            cols = pl.ds(pl.multiple_of(core * half + j * LAT, 128), LAT)
            value = total[:, j * LAT : (j + 1) * LAT] / tally
            climate[rows, cols] = value
            zonal_sum = zonal_sum + value
        zhalf[rows, :] = zonal_sum
        third.append(pltpu.make_async_remote_copy(
            src_ref=climate.at[rows, mine], dst_ref=climate.at[rows, mine], send_sem=tsem.at[s],
            recv_sem=tsem.at[3 + s], device_id={"tm": partner}, device_id_type=MESH,
        ))
        if s < 2:
            third[s].start()

    quarter = climate.shape[0] // 4
    swap = pltpu.make_async_remote_copy(
        src_ref=zhalf.at[pl.ds(pl.multiple_of(partner * quarter, 8), quarter)], dst_ref=zother,
        send_sem=xsem.at[0], recv_sem=xsem.at[1], device_id={"tm": partner}, device_id_type=MESH,
    )
    swap.start()
    third[2].start()
    if zrows > quarter:
        zpart[quarter:, :] = jnp.zeros((zrows - quarter, LAT), F32)
    swap.wait()
    zpart[:quarter, :] = zhalf[pl.ds(pl.multiple_of(tm * quarter, 8), quarter), :] + zother[...]
    copies = []
    for k in range(1, n):
        peer = lax.rem(me + k, n)
        copy = pltpu.make_async_remote_copy(
            src_ref=zpart.at[pl.ds(pl.multiple_of(peer * share, 8), share)],
            dst_ref=zbox.at[k - 1], send_sem=zsend.at[k - 1], recv_sem=zrecv.at[k - 1],
            device_id={"cells": peer}, device_id_type=MESH,
        )
        copy.start()
        copies.append(copy)
    block = pl.ds(pl.multiple_of(me * share, 8), share)
    total = zpart[block, :]
    for k in range(1, n):
        copies[k - 1].wait_recv()
        total = total + zbox[k - 1]
    zonal[tm, block, :] = total / lon_total
    gathers = []
    for k in range(1, n):
        copy = pltpu.make_async_remote_copy(
            src_ref=zonal.at[tm, block], dst_ref=zonal.at[tm, block],
            send_sem=gsend.at[k - 1], recv_sem=grecv.at[k - 1],
            device_id={"cells": lax.rem(me + k, n)}, device_id_type=MESH,
        )
        copy.start()
        gathers.append(copy)
    for k in range(1, n):
        copies[k - 1].wait_send()
        gathers[k - 1].wait_send()
        source = lax.rem(me + n - k, n)
        there = zonal.at[tm, pl.ds(pl.multiple_of(source * share, 8), share)]
        pltpu.make_async_remote_copy(
            src_ref=there, dst_ref=there, send_sem=gsend.at[k - 1], recv_sem=grecv.at[k - 1],
            device_id={"cells": source}, device_id_type=MESH,
        ).wait_recv()
    spreads = []
    for k in range(1, 4):
        copy = pltpu.make_async_remote_copy(
            src_ref=zonal.at[tm], dst_ref=zonal.at[tm],
            send_sem=tsend.at[k - 1], recv_sem=trecv.at[k - 1],
            device_id={"tm": lax.rem(tm + k, 4)}, device_id_type=MESH,
        )
        copy.start()
        spreads.append(copy)
    for k in range(1, 4):
        spreads[k - 1].wait_send()
        source = lax.rem(tm + 4 - k, 4)
        pltpu.make_async_remote_copy(
            src_ref=zonal.at[source], dst_ref=zonal.at[source],
            send_sem=tsend.at[k - 1], recv_sem=trecv.at[k - 1],
            device_id={"tm": source}, device_id_type=MESH,
        ).wait_recv()
    for copy in sends:
        copy.wait_send()
    for s, rows in enumerate(parts):
        first[s].wait_send()
        second[s].wait_send()
        third[s].wait_send()
        pltpu.make_async_remote_copy(
            src_ref=climate.at[rows, theirs], dst_ref=climate.at[rows, theirs], send_sem=tsem.at[s],
            recv_sem=tsem.at[3 + s], device_id={"tm": partner}, device_id_type=MESH,
        ).wait_recv()


def local(geopotential, meridional, day_index):
    frames, width = geopotential.shape
    n = lax.axis_size("cells")
    lon_total = width // LAT * n
    step = 16 * n
    count = 4
    pieces, base = [], 0
    for p in range(count):
        rows = 2 * (frames // count) + (4 * EDGE if p == 0 else 0)
        rows = -(-rows // step) * step
        pieces.append((base, rows))
        base += rows
    share = max(rows for _, rows in pieces) // n
    quarter = 3 * DROWS // 4
    zshare = -(-quarter // (8 * n)) * 8
    zrows = n * zshare
    half = width // 2

    dma = pltpu.SemaphoreType.DMA
    climate, zonal = pl.pallas_call(
        functools.partial(eddy_kernel, n, float(lon_total), zrows, pieces),
        out_shape=(
            jax.ShapeDtypeStruct((3 * DROWS, width), F32),
            jax.ShapeDtypeStruct((4, zrows, LAT), F32),
        ),
        in_specs=[pl.BlockSpec(memory_space=pl.ANY)] * 2 + [vmem()] * 2,
        out_specs=(vmem(), vmem()),
        scratch_shapes=[
            pltpu.VMEM((frames, width), BF16),
            pltpu.VMEM((frames, width), BF16),
            pltpu.VMEM((2, 2 * EDGE, width), BF16),
            pltpu.VMEM((base, LAT), BF16),
            pltpu.VMEM((count, n - 1, share, LAT), BF16),
            pltpu.VMEM((base, LAT), F32),
            pltpu.VMEM((frames + 2 * EDGE, 2 * width), BF16),
            pltpu.VMEM((frames, 3 * width), BF16),
            pltpu.VMEM((DROWS, frames), BF16),
            pltpu.VMEM((8, DROWS), F32),
            pltpu.VMEM((3 * DROWS, half), F32),
            pltpu.VMEM((3 * DROWS, half), F32),
            pltpu.VMEM((3 * DROWS, half), F32),
            pltpu.VMEM((3 * DROWS, half), BF16),
            pltpu.VMEM((3 * DROWS, half), BF16),
            pltpu.VMEM((3, 8, DROWS), F32),
            pltpu.VMEM((3 * DROWS, LAT), F32),
            pltpu.VMEM((quarter, LAT), F32),
            pltpu.VMEM((zrows, LAT), F32),
            pltpu.VMEM((n - 1, zshare, LAT), F32),
            dma((2 * count,)), dma((8,)),
            dma((count, n - 1)), dma((count, n - 1)),
            dma((count, n // 2 - 1)), dma((count, n // 2 - 1)), dma((count, n // 2)), dma((count, n // 2)),
            dma((6,)), dma((6,)), dma((6,)), dma((6,)), dma((2,)),
            dma((n - 1,)), dma((n - 1,)), dma((n - 1,)), dma((n - 1,)),
            dma((3,)), dma((3,)),
        ],
        compiler_params=pltpu.CompilerParams(collective_id=0, has_side_effects=True, vmem_limit_bytes=LIMIT),
    )(geopotential, meridional, day_index.reshape(1, frames), taps_matrix())
    climate = climate.reshape(3, DROWS, width)[:, :DAYS]
    zonal = zonal[:, :quarter].reshape(3, DROWS, LAT)[:, :DAYS]
    return (climate, zonal)


def solution(mesh):
    return jax.shard_map(
        local,
        mesh=mesh,
        in_specs=(P("tm", "cells"), P("tm", "cells"), P("tm")),
        out_specs=(P(None, None, "cells"), P()),
        check_vma=False,
    )
```

time: 147 us -> 122 us (0.83)
  Pallas kernels: 139 us -> 116 us
    pallas_call x3 -> x1, Pallas kernels: 139 us -> 116 us  [local(): pl.pallas_call(functools.partial(eddy_kernel, n, float(lon_total), zrows,...]
    unnamed x6 -> x4, local copies, waits for them, and re-layouts: 3.48 us -> 2.58 us
where the time goes in v3:
time: 122 us
  Pallas kernels  116 us (95%)
  local copies, waits for them, and re-layouts  5.74 us (5%)
    pallas_call x1, Pallas kernels, local(): pl.pallas_call(functools.partial(eddy_kernel, n, float(lon_total), zrows,...  116 us
    unnamed x4, local copies, waits for them, and re-layouts  2.58 us

profile of v3, /device:TPU:1, one launch (start us, length us, event | category | flops | bytes accessed | tf_op | source)
XLA Modules:
  0.0 122.1 jit_solution(5886393207741010090)
XLA Ops:
  0.6 0.7 reshape.13.days
  1.3 0.0 copy-start
  1.3 1.7 %copy-done = bf16[2560,512]{1,0:T(8,128)(2,1)S(1)} copy-done((bf16[2560,512]{1,0:T(8,128)(2,1)S(1)}, bf16[2560,512]{1,0:T(8,128)(2,1)}, u32[]{:S(2)}) %copy-start) | copy-done | bytes 2621464
  3.1 0.0 copy-start.1
  3.1 0.8 copy-done.1
  3.9 115.7 %shard_map.59 = (f32[1152,512]{1,0:T(8,128)S(1)}, f32[4,320,128]{2,1,0:T(8,128)S(1)}) custom-call(bf16[2560,512]{1,0:T(8,128)(2,1)S(1)} %copy-done, bf16[2560,512]{1,0:T(8,128)(2,1)} %mer_in.1, s32[1,2560]{1,0:T(1,128)S(1)} %reshape.13.days, bf16[128,160]{1,0:T(8,128)(2,1)S(1)} %copy-done.1), custom_call_target="tpu_custom_call" | custom-call | tf_op jit(solution)/shard_map/pallas_call | solution.py:394
  119.7 1.6 %slice.12 = f32[3,365,512]{2,1,0:T(8,128)} slice(f32[3,384,512]{2,1,0:T(8,128)S(1)} %bitcast.2), slice={[0:3], [0:365], [0:512]} | slice | bytes 4485120 | tf_op jit(solution)/shard_map/slice | solution.py:432
  121.3 0.8 slice.13
  (1 shorter events, 0.0 us)
Async XLA Ops:
  1.3 1.7 %copy-start = (bf16[2560,512]{1,0:T(8,128)(2,1)S(1)}, bf16[2560,512]{1,0:T(8,128)(2,1)}, u32[]{:S(2)}) copy-start(bf16[2560,512]{1,0:T(8,128)(2,1)} %geo_in.1) | copy-start | bytes 7864324
  3.1 0.8 copy-start.1

commit v4 on v3

--- a/solution.py
+++ b/solution.py
@@ -16,7 +16,7 @@
 EDGE = 16
 TILE = 128
 SLAB = TILE + 2 * EDGE
-LIMIT = 48 * 1024 * 1024
+LIMIT = 60 * 1024 * 1024
 MESH = pl.DeviceIdType.MESH
 F32 = jnp.float32
 BF16 = jnp.bfloat16
@@ -143,12 +143,38 @@
             scattered[p].append(copy)
             sends.append(copy)
 
+    place = lax.div(me, 2)
+
     def spread(p, source, peer, send_sem, recv_sem):
         rows = mean.at[chunk(p, source)]
         return pltpu.make_async_remote_copy(
             src_ref=rows, dst_ref=rows, send_sem=send_sem, recv_sem=recv_sem,
             device_id={"cells": peer}, device_id_type=MESH,
         )
+
+    def hop(p, side, j):
+        sign = 1 - 2 * side
+        return spread(p, me - 2 * sign * j, me + 2 * sign, gssem.at[side, p, j], grsem.at[side, p, j])
+
+    def arrival(p, side, j):
+        sign = 1 - 2 * side
+        return spread(p, me - 2 * sign * j, me - 2 * sign, gssem.at[side, p, j - 1], grsem.at[side, p, j - 1])
+
+    def handing(p, side, j):
+        sign = 1 - 2 * side
+        slot = side * (m - 1) + j
+        return spread(p, me - 2 * sign * j, mate, fssem.at[p, slot], frsem.at[p, slot])
+
+    def handed(p, side, j):
+        sign = 1 - 2 * side
+        slot = side * (m - 1) + j
+        return spread(p, mate - 2 * sign * j, mate, fssem.at[p, slot], frsem.at[p, slot])
+
+    def has(side, j):
+        return place >= j if side == 0 else place + j < m
+
+    def onward(side):
+        return has(1 - side, 1)
 
     def reduce(p):
         size = pieces[p][1] // n
@@ -158,26 +184,55 @@
             scattered[p][k - 1].wait_recv()
             total = total + mbox[p, k - 1, :size].astype(F32)
         mean[mine, :] = total / lon_total
-        copy = spread(p, me, mate, fssem.at[p, 0], frsem.at[p, 0])
-        copy.start()
-        sends.append(copy)
-        for k in range(1, m):
-            copy = spread(p, me, lax.rem(me + 2 * k, n), gssem.at[p, k - 1], grsem.at[p, k - 1])
-            copy.start()
-            sends.append(copy)
+        handing(p, 0, 0).start()
+        for side in range(2):
+
+            @pl.when(onward(side))
+            def _():
+                hop(p, side, 0).start()
 
     def forward(p):
-        for k in range(1, m):
-            source = lax.rem(me + n - 2 * k, n)
-            spread(p, source, source, gssem.at[p, k - 1], grsem.at[p, k - 1]).wait_recv()
-            copy = spread(p, source, mate, fssem.at[p, k], frsem.at[p, k])
-            copy.start()
-            sends.append(copy)
+        for j in range(1, m):
+            for side in range(2):
+
+                @pl.when(has(side, j))
+                def _():
+                    arrival(p, side, j).wait_recv()
+                    handing(p, side, j).start()
+                    if j < m - 1:
+
+                        @pl.when(onward(side))
+                        def _():
+                            hop(p, side, j).start()
 
     def settle(p):
-        for k in range(m):
-            source = lax.rem(mate + n - 2 * k, n)
-            spread(p, source, mate, fssem.at[p, k], frsem.at[p, k]).wait_recv()
+        handed(p, 0, 0).wait_recv()
+        for j in range(1, m):
+            for side in range(2):
+
+                @pl.when(has(side, j))
+                def _():
+                    handed(p, side, j).wait_recv()
+
+    def finish(p):
+        handing(p, 0, 0).wait_send()
+        for side in range(2):
+
+            @pl.when(onward(side))
+            def _():
+                hop(p, side, 0).wait_send()
+
+        for j in range(1, m):
+            for side in range(2):
+
+                @pl.when(has(side, j))
+                def _():
+                    handing(p, side, j).wait_send()
+                    if j < m - 1:
+
+                        @pl.when(onward(side))
+                        def _():
+                            hop(p, side, j).wait_send()
 
     def put(field, dst, block, value):
         for j in range(lons):
@@ -362,6 +417,8 @@
         ).wait_recv()
     for copy in sends:
         copy.wait_send()
+    for p in range(count):
+        finish(p)
     for s, rows in enumerate(parts):
         first[s].wait_send()
         second[s].wait_send()
@@ -377,7 +434,7 @@
     n = lax.axis_size("cells")
     lon_total = width // LAT * n
     step = 16 * n
-    count = 4
+    count = 5
     pieces, base = [], 0
     for p in range(count):
         rows = 2 * (frames // count) + (4 * EDGE if p == 0 else 0)
@@ -422,7 +479,7 @@
             pltpu.VMEM((n - 1, zshare, LAT), F32),
             dma((2 * count,)), dma((8,)),
             dma((count, n - 1)), dma((count, n - 1)),
-            dma((count, n // 2 - 1)), dma((count, n // 2 - 1)), dma((count, n // 2)), dma((count, n // 2)),
+            dma((2, count, n // 2 - 1)), dma((2, count, n // 2 - 1)), dma((count, n - 1)), dma((count, n - 1)),
             dma((6,)), dma((6,)), dma((6,)), dma((6,)), dma((2,)),
             dma((n - 1,)), dma((n - 1,)), dma((n - 1,)), dma((n - 1,)),
             dma((3,)), dma((3,)),

time: 122 us -> 122 us (level)
    unnamed x4 -> x2, local copies, waits for them, and re-layouts: 2.58 us -> 0.01 us
    slice x1, local copies, waits for them, and re-layouts: 1.57 us -> 3.27 us  [local(): climate = climate.reshape(3, DROWS, width)[:, :DAYS]]
where the time goes in v4:
time: 122 us; the launch traced here: 121 us
  Pallas kernels  115 us (94%)
  local copies, waits for them, and re-layouts  5.47 us (4%)
    pallas_call x1, Pallas kernels, local(): pl.pallas_call(functools.partial(eddy_kernel, n, float(lon_total), zrows,...  115 us
    slice x1, local copies, waits for them, and re-layouts, local(): climate = climate.reshape(3, DROWS, width)[:, :DAYS]  3.27 us

profile of v4, /device:TPU:1, one launch (start us, length us, event | category | flops | bytes accessed | tf_op | source)
XLA Modules:
  0.0 121.3 jit_solution(543393293200826277)
XLA Ops:
  0.6 1.3 %reshape.13.days = s32[1,2560]{1,0:T(1,128)} reshape(s32[2560]{0:T(1024)} %param.6) | data formatting | bytes 20480 | tf_op jit(solution)/shard_map/reshape | solution.py:488
  1.9 115.1 %shard_map.59 = (f32[1152,512]{1,0:T(8,128)}, f32[4,320,128]{2,1,0:T(8,128)}) custom-call(bf16[2560,512]{1,0:T(8,128)(2,1)} %geo_in.1, bf16[2560,512]{1,0:T(8,128)(2,1)} %mer_in.1, s32[1,2560]{1,0:T(1,128)} %reshape.13.days, bf16[128,160]{1,0:T(8,128)(2,1)} %constant.3.taps), custom_call_target="tpu_custom_call" | custom-call | tf_op jit(solution)/shard_map/pallas_call | solution.py:451
  117.1 0.0 copy-start
  117.1 3.3 %slice.12 = f32[3,365,512]{2,1,0:T(8,128)} slice(f32[3,384,512]{2,1,0:T(8,128)} %bitcast.3), slice={[0:3], [0:365], [0:512]} | slice | bytes 4485120 | tf_op jit(solution)/shard_map/slice | solution.py:489
  120.4 0.0 copy-done
  120.4 0.8 slice.13
  (1 shorter events, 0.0 us)
Async XLA Ops:
  117.1 3.3 %copy-start = (f32[4,320,128]{2,1,0:T(8,128)S(1)}, f32[4,320,128]{2,1,0:T(8,128)}, u32[]{:S(2)}) copy-start(f32[4,320,128]{2,1,0:T(8,128)} %get-tuple-element.5) | copy-start | bytes 1966084

commit v5 on v4

--- a/solution.py
+++ b/solution.py
@@ -271,12 +271,12 @@
                 products[pl.ds(r, TILE), 2 * width + a0 : 2 * width + a1] = (a * b).astype(BF16)
 
     tell = []
-    for t in range(count + 3):
+    for t in range(count + 4):
         if t < count:
             lanes(t)
             scatter(t)
-        if 1 <= t <= count:
-            if t == 1:
+        if 2 <= t <= count + 1:
+            if t == 2:
 
                 @pl.loop(0, frames // TILE)
                 def _(i):
@@ -294,19 +294,21 @@
                     )
                     copy.start()
                     tell.append(copy)
-            reduce(t - 1)
-        if 2 <= t <= count + 1:
-            forward(t - 2)
-        if t >= 3:
-            settle(t - 3)
-            anomalies(t - 3)
-            filtering(t - 3)
+            reduce(t - 2)
+        if 3 <= t <= count + 2:
+            forward(t - 3)
+        if t >= 4:
+            settle(t - 4)
+            anomalies(t - 4)
+            filtering(t - 4)
 
     mine = pl.ds(pl.multiple_of(core * half, 128), half)
     theirs = pl.ds(pl.multiple_of((1 - core) * half, 128), half)
     parts = [slice(s * DROWS, (s + 1) * DROWS) for s in range(3)]
     first, second, third = [], [], []
-    for s, rows in enumerate(parts):
+
+    def hand_over(s):
+        rows = parts[s]
         cols = pl.ds(pl.multiple_of(s * width + (1 - core) * half, 128), half)
         give[rows, :] = jnp.dot(onehot[...], products[:, cols], preferred_element_type=F32)
         first.append(pltpu.make_async_remote_copy(
@@ -314,9 +316,13 @@
             device_id={"tm": partner}, device_id_type=MESH,
         ))
         first[s].start()
+
+    hand_over(0)
     for s, rows in enumerate(parts):
         cols = pl.ds(pl.multiple_of(s * width + core * half, 128), half)
         keep[rows, :] = jnp.dot(onehot[...], products[:, cols], preferred_element_type=F32)
+        if s < 2:
+            hand_over(s + 1)
         first[s].wait_recv()
         own[rows, :] = (keep[rows, :] + inbox[rows, :]).astype(BF16)
         second.append(pltpu.make_async_remote_copy(

time: 122 us -> 121 us (level)
  no operation moved by 1% of the time
where the time goes in v5:
time: 121 us
  Pallas kernels  115 us (95%)
  local copies, waits for them, and re-layouts  5.47 us (5%)
    pallas_call x1, Pallas kernels, local(): pl.pallas_call(functools.partial(eddy_kernel, n, float(lon_total), zrows,...  115 us
    slice x1, local copies, waits for them, and re-layouts, local(): climate = climate.reshape(3, DROWS, width)[:, :DAYS]  3.27 us

profile of v5, /device:TPU:1, one launch (start us, length us, event | category | flops | bytes accessed | tf_op | source)
XLA Modules:
  0.0 120.7 jit_solution(12232550808918942121)
XLA Ops:
  0.6 1.3 %reshape.13.days = s32[1,2560]{1,0:T(1,128)} reshape(s32[2560]{0:T(1024)} %param.6) | data formatting | bytes 20480 | tf_op jit(solution)/shard_map/reshape | solution.py:494
  1.9 114.6 %shard_map.59 = (f32[1152,512]{1,0:T(8,128)}, f32[4,320,128]{2,1,0:T(8,128)}) custom-call(bf16[2560,512]{1,0:T(8,128)(2,1)} %geo_in.1, bf16[2560,512]{1,0:T(8,128)(2,1)} %mer_in.1, s32[1,2560]{1,0:T(1,128)} %reshape.13.days, bf16[128,160]{1,0:T(8,128)(2,1)} %constant.3.taps), custom_call_target="tpu_custom_call" | custom-call | tf_op jit(solution)/shard_map/pallas_call | solution.py:457
  116.5 0.0 copy-start
  116.6 3.3 %slice.12 = f32[3,365,512]{2,1,0:T(8,128)} slice(f32[3,384,512]{2,1,0:T(8,128)} %bitcast.3), slice={[0:3], [0:365], [0:512]} | slice | bytes 4485120 | tf_op jit(solution)/shard_map/slice | solution.py:495
  119.8 0.0 copy-done
  119.9 0.8 slice.13
  (1 shorter events, 0.0 us)
Async XLA Ops:
  116.5 3.3 %copy-start = (f32[4,320,128]{2,1,0:T(8,128)S(1)}, f32[4,320,128]{2,1,0:T(8,128)}, u32[]{:S(2)}) copy-start(f32[4,320,128]{2,1,0:T(8,128)} %get-tuple-element.5) | copy-start | bytes 1966084
